TPU v7x, 32 devices: a whole 2x2x4 slice. The times are simulated.
32 devices in a mesh: lat: 4 (over z), lon: 8 (over y, x, core).
Axes of the slice: x: 2, y: 2, z: 4, core: 2. Of those that a mesh axis runs over, the one named last changes fastest.
Arguments:
- sigma: float32 [4, 512, 1024], P(None, 'lat', 'lon'), may hold values from 0.5 to 2
- east_coef: float32 [4, 512, 1024], P(None, 'lat', 'lon'), may hold values from 0.04 to 0.24
- north_coef: float32 [4, 512, 1024], P(None, 'lat', 'lon'), may hold values from 0.04 to 0.24
- mask: int32 [4, 512, 1024], P(None, 'lat', 'lon'), may hold values 0 or 1
- innovations: float32 [4096, 128], P(('lat', 'lon')), may hold values from -6 to 6
- cells: int32 [4096, 128], P(('lat', 'lon')), may hold values from 0 to 65535
- owner: int32 [4096, 1], P(('lat', 'lon')), may hold values from 0 to 31; in each aligned block of 128 rows (0 to 127, 128 to 255, ...) at most 8 rows name the same one
- obs_weights: float32 [4096, 128, 128], P(('lat', 'lon')), may hold values from 0 to 4, as said below
Outputs:
- increment: float32 [4, 512, 1024], P(None, 'lat', 'lon')
- residual: float32 [4, 512, 1024], P(None, 'lat', 'lon')
Inputs may be any that keep to these rules, and one draw needn't show every extreme that they name: `owner`: within the 128 blocks held by one device, no tile is named by more than 8 blocks, a bound that some block reaches. `obs_weights`: each block is symmetric and positive definite.
All inputs are finite; a program needn't handle non-finite values. No bound on the sum of `mask` on one device may be relied on, other than what follows from the above.
Results may differ from a plain program's by a relative error of at most 0.0003.
Values sent between devices are 32-bit elements; how exact they have to be, the bound alone decides.
No kernel may reach another device: no remote copies, remote signals or barrier semaphores. Data moves between devices by JAX's collectives and lax.ppermute only.
A program may use at most 128 MiB of HBM per device.

v0:
```python
import functools

import jax
import jax.numpy as jnp
from jax import lax
from jax.experimental import pallas as pl
from jax.experimental.pallas import tpu as pltpu
from jax.sharding import PartitionSpec as P

PASSES = 5
HALO = 16
EDGE = 8
GROUP = 16
CHUNK = 16
AHEAD = 4
F32 = jnp.float32
BF16 = jnp.bfloat16
VMEM = pl.BlockSpec(memory_space=pltpu.VMEM)
HBM = pl.BlockSpec(memory_space=pltpu.HBM)
SMEM = pl.BlockSpec(memory_space=pltpu.SMEM)
PARAMS = pltpu.CompilerParams(vmem_limit_bytes=32 * 1024 * 1024)

ROOMLESS = pltpu.CompilerParams(vmem_limit_bytes=60 * 1024 * 1024)


SNUG = pltpu.CompilerParams(vmem_limit_bytes=52 * 1024 * 1024)


def parts(values):
    high = values.astype(BF16)
    low = (values - high.astype(F32)).astype(BF16)
    return high, low


def lane_of(rows):
    return lax.broadcasted_iota(jnp.int32, (rows, 128), 1)


def pack_sides(fields):
    lane = lane_of(fields[0].shape[0])
    packed = jnp.zeros_like(fields[0])
    for level, field in enumerate(fields):
        start = 2 * HALO * level
        turned = pltpu.roll(field, (start + HALO) % 128, 1)
        packed = jnp.where((lane >= start) & (lane < start + 2 * HALO), turned, packed)
    return packed


def turn_kernel(count, *refs):
    sources, extra = refs[: 3 * count], refs[3 * count : len(refs) - count - 2]
    *mixed, down, up = refs[len(refs) - count - 2 :]
    row = 0
    if extra:
        row = extra[0].shape[0]
        down[0:row] = extra[0][...]
        up[0:row] = extra[1][...]
    for index in range(count):
        fields, from_east, from_west = sources[3 * index : 3 * index + 3]
        levels, rows, _ = fields.shape[-3:]
        western = lane_of(rows) % (2 * HALO) < HALO
        for at in [(i,) for i in range(fields.shape[0])] if len(fields.shape) == 4 else [()]:
            sides = jnp.where(western, from_west[at + (...,)], from_east[at + (...,)])
            mixed[index][at + (...,)] = sides
            for level in range(levels):
                down[row, level] = fields[at + (level, slice(rows - HALO, rows))]
                up[row, level] = fields[at + (level, slice(0, HALO))]
            down[row, levels] = sides[rows - HALO :]
            up[row, levels] = sides[:HALO]
            row += 1


def exchange(fields, sides):
    mixed, down, up = turn((fields, *exchange_columns(sides)))
    return (*exchange_rows(down, up), mixed)


def exchange_columns(sides):
    wide = lax.axis_size("lon")
    east = [(i, (i + 1) % wide) for i in range(wide)]
    from_west = lax.ppermute(sides, "lon", east)
    from_east = lax.ppermute(sides, "lon", [(to, at) for at, to in east])
    return from_east, from_west


def turn(*groups, rows_ahead=()):
    levels, rows, cols = groups[0][0].shape[-3:]
    shapes = [sides.shape for _, sides, _ in groups]
    total = sum(fields.shape[0] if fields.ndim == 4 else 1 for fields, _, _ in groups)
    total += rows_ahead[0].shape[0] if rows_ahead else 0
    shapes += [(total, levels + 1, HALO, cols)] * 2
    return pl.pallas_call(
        functools.partial(turn_kernel, len(groups)),
        out_shape=[jax.ShapeDtypeStruct(shape, F32) for shape in shapes],
        in_specs=[VMEM] * (3 * len(groups) + len(rows_ahead)),
        out_specs=[VMEM] * len(shapes),
        compiler_params=PARAMS,
        name="turn",
    )(*[array for group in groups for array in group], *rows_ahead)


def exchange_rows(down, up):
    tall = lax.axis_size("lat")
    first = [(i, i + 1) for i in range(0, tall - 1, 2)]
    second = [(i, i + 1) for i in range(1, tall - 1, 2)]
    even = lax.axis_index("lat") % 2 == 0
    one = lax.ppermute(
        jnp.where(even, down, up), "lat", first + [(to, at) for at, to in first]
    )
    two = lax.ppermute(
        jnp.where(even, up, down), "lat", second + [(to, at) for at, to in second]
    )
    return jnp.where(even, two, one), jnp.where(even, one, two)


def neighbours(tiles):
    lane = lane_of(tiles[0].shape[0])
    later, earlier = tiles[1:] + tiles[:1], tiles[-1:] + tiles[:-1]
    after = [
        pltpu.roll(jnp.where(lane == 0, other, tile), 127, 1) for tile, other in zip(tiles, later)
    ]
    before = [
        pltpu.roll(jnp.where(lane == 127, other, tile), 1, 1) for tile, other in zip(tiles, earlier)
    ]
    return after, before


def lay_out(fields, side):
    lane = lane_of(side.shape[0])
    width = 2 * HALO
    turned = [pltpu.roll(field, width * level + HALO, 1) for level, field in enumerate(fields)]
    tiles = []
    for tile in range(len(fields) + 1):
        left, right = width * tile - HALO, width * tile + HALO
        before = turned[tile - 1] if tile else turned[0]
        after = turned[tile] if tile < len(fields) else turned[-1]
        value = jnp.where(lane < left, before, after)
        tiles.append(jnp.where((lane >= left) & (lane < right), side, value))
    return tiles


def pick_out(first, second, level):
    start = 2 * HALO * level + HALO
    return pltpu.roll(jnp.where(lane_of(first.shape[0]) >= start, first, second), 128 - start, 1)


def place(target, own, halo, row, lead=()):
    before, after, mixed = halo
    levels = before.shape[-3] - 1
    rows = mixed.shape[-2]
    spans = (
        (EDGE, before, (row,), before[row, levels]),
        (EDGE + HALO, own, lead, mixed[lead + (...,)]),
        (EDGE + HALO + rows, after, (row,), after[row, levels]),
    )
    for start, source, at, side in spans:
        tiles = lay_out([source[at + (level,)] for level in range(levels)], side)
        for tile, value in enumerate(tiles):
            target[lead + (tile, slice(start, start + side.shape[0]))] = value
    blank = jnp.zeros((EDGE, 128), F32)
    for tile in range(levels + 1):
        target[lead + (tile, slice(0, EDGE))] = blank
        target[lead + (tile, slice(EDGE + 2 * HALO + rows, 2 * EDGE + 2 * HALO + rows))] = blank


def clear_margins(target):
    blank = jnp.zeros((target.shape[0], EDGE, 128), F32)
    target[:, 0:EDGE] = blank
    target[:, target.shape[1] - EDGE :] = blank


def face_kernel(products, before, after, mixed, weights, padded, faces):
    tiles, tall = weights.shape[1:3]
    for index in range(2):
        place(padded, products, (before, after, mixed), index, (index,))
    inner = slice(EDGE, EDGE + tall)
    faces[:, 0:EDGE] = jnp.zeros((tiles, EDGE, 128), F32)
    faces[:, EDGE + tall :] = jnp.zeros((tiles, EDGE, 128), F32)
    land = [(padded[0, tile, inner] > 0.0).astype(F32) for tile in range(tiles)]
    land_east, _ = neighbours(land)
    east_face = [padded[0, tile, inner] * land_east[tile] for tile in range(tiles)]
    _, west_face = neighbours(east_face)
    for tile in range(tiles):
        land_north = (padded[0, tile, EDGE + 1 : EDGE + 1 + tall] > 0.0).astype(F32)
        north_face = padded[1, tile, inner] * land_north
        faces[tile, inner] = north_face
        south_face = faces[tile, EDGE - 1 : EDGE - 1 + tall]
        weights[0, tile] = 1.0 - (
            ((east_face[tile] + west_face[tile]) + north_face) + south_face
        )
        weights[1, tile] = east_face[tile]
        weights[2, tile] = west_face[tile]
        weights[3, tile] = north_face
        weights[4, tile] = south_face


def face_weights(products, halo):
    _, levels, rows, cols = products.shape
    tall = rows + 2 * HALO
    return pl.pallas_call(
        face_kernel,
        out_shape=jax.ShapeDtypeStruct((5, levels + 1, tall, cols), F32),
        in_specs=[VMEM] * 4,
        out_specs=VMEM,
        scratch_shapes=[
            pltpu.VMEM((2, levels + 1, tall + 2 * EDGE, cols), F32),
            pltpu.VMEM((levels + 1, tall + 2 * EDGE, cols), F32),
        ],
        compiler_params=PARAMS,
        name="face_weights",
    )(products, *halo)


def sweep(source, target, weights, rows_from, rows_to, block):
    tiles = source.shape[0]

    def step(index, carry):
        first = pl.multiple_of(rows_from + index * block, 8)
        for start in range(0, block, 16):
            count = min(16, block - start)
            at = pl.multiple_of(first + EDGE + start, 8)
            inner = pl.ds(pl.multiple_of(first + start, 8), count)
            here = [source[tile, pl.ds(at, count)] for tile in range(tiles)]
            east, west = neighbours(here)
            for tile in range(tiles):
                above = source[tile, pl.ds(at + 1, count)]
                below = source[tile, pl.ds(at - 1, count)]
                total = weights[0, tile, inner] * here[tile]
                total += weights[1, tile, inner] * east[tile]
                total += weights[2, tile, inner] * west[tile]
                total += weights[3, tile, inner] * above
                total += weights[4, tile, inner] * below
                target[tile, pl.ds(at, count)] = total
        return carry

    lax.fori_loop(0, (rows_to - rows_from) // block, step, 0)


def smooth(field, spare, weights, skip, block, paired):
    tall = weights.shape[2]

    def two(index, carry):
        sweep(field, spare, weights, skip, tall - skip, block)
        sweep(spare, field, weights, skip, tall - skip, block)
        return carry

    if paired:
        lax.fori_loop(0, PASSES // 2, two, 0)
    else:
        for index in range(PASSES // 2):
            two(index, 0)
    sweep(field, spare, weights, skip, tall - skip, block)
    return field, spare


def index_iota(cells):
    return lax.broadcasted_iota(jnp.int32, (cells, 128), 0).astype(F32).astype(BF16)


def spread_row(row, count):
    return jnp.broadcast_to(jnp.broadcast_to(row, (16, 128)).astype(BF16)[0:1], (count, 128))


def one_hot(iota, row):
    count = iota.shape[0]
    return jnp.where(
        iota == spread_row(row, count), jnp.ones((count, 128), BF16), jnp.zeros((count, 128), BF16)
    )


def scatter_into(total, load_rows, slots, half_rows, half_cols, group):
    row_iota = index_iota(half_rows)
    col_iota = index_iota(half_cols)
    total[...] = jnp.zeros_like(total)

    def step(index, carry):
        high_rows, low_rows, columns = [], [], []
        for row_index, col_index, value in load_rows(index):
            high, low = parts(jnp.broadcast_to(value, (16, 128)))
            high = jnp.broadcast_to(high[0:1], (half_rows, 128))
            low = jnp.broadcast_to(low[0:1], (half_rows, 128))
            hit = row_iota == spread_row(row_index, half_rows)
            zero = jnp.zeros((half_rows, 128), BF16)
            high_rows.append(jnp.where(hit, high, zero))
            low_rows.append(jnp.where(hit, low, zero))
            columns.append(one_hot(col_iota, col_index))
        left = jnp.concatenate(high_rows + low_rows, axis=1)
        right = jnp.concatenate(columns + columns, axis=1)
        total[...] += lax.dot_general(
            left, right, (((1,), (1,)), ((), ())), preferred_element_type=F32
        )
        return carry

    lax.fori_loop(0, slots // group, step, 0)


def load_group(index, group, capacity, row_at, col_at, arrived, stride, first_slot):
    base = pl.multiple_of(index * group, group)
    row_block = row_at[pl.ds(base, group)]
    col_block = col_at[pl.ds(base, group)]
    for j in range(group):
        source = index * (group // capacity) + j // capacity
        at = source * stride + first_slot + j % capacity
        yield row_block[j : j + 1], col_block[j : j + 1], arrived[pl.ds(at, 1)]


def split_cells(cells, rows, cols):
    level = cells // (rows * cols)
    row = (cells // cols) % rows
    col = cells % cols
    return (level // 2) * rows + row, (level % 2) * cols + col


def put_field(total, sigma, field, extra=None):
    levels, rows, cols = sigma.shape
    fields = []
    for level in range(levels):
        r, c = level // 2 * rows, level % 2 * cols
        value = total[r : r + rows, c : c + cols]
        value = sigma[level] * value
        if extra is not None:
            value = value + extra(level)
        field[level] = value
        fields.append(value)
    return fields


def scatter_first_kernel(capacity, arrived, sigma, row_at, col_at, field, *refs):
    sides, total = refs
    levels, rows, cols = sigma.shape
    stride = 2 * capacity
    cells = jnp.concatenate(
        [arrived[at : at + capacity] for at in range(0, arrived.shape[0], stride)], axis=0
    )
    row_index, col_index = split_cells(cells.astype(jnp.int32), rows, cols)
    row_at[...] = row_index.astype(F32)
    col_at[...] = col_index.astype(F32)

    def load(index):
        return load_group(index, 64, capacity, row_at, col_at, arrived, stride, capacity)

    scatter_into(total, load, row_at.shape[0], levels // 2 * rows, 2 * cols, 64)
    sides[...] = pack_sides(put_field(total, sigma, field))


def scatter_first(arrived, sigma, capacity):
    levels, rows, cols = sigma.shape
    slots = arrived.shape[0] // 2
    shapes = [(slots, 128), (slots, 128), (levels, rows, cols), (rows, cols)]
    out = pl.pallas_call(
        functools.partial(scatter_first_kernel, capacity),
        out_shape=[jax.ShapeDtypeStruct(shape, F32) for shape in shapes],
        in_specs=[VMEM] * 2,
        out_specs=[VMEM] * len(shapes),
        scratch_shapes=[pltpu.VMEM((levels // 2 * rows, 2 * cols), F32)],
        compiler_params=PARAMS,
        name="scatter_first",
    )(arrived, sigma)
    return out


def lane_value(block, lane):
    return jnp.sum(jnp.where(lane_of(block.shape[0]) == lane, block, 0.0))


def lanes(values, rows):
    lane = lane_of(rows)
    out = jnp.zeros((rows, 128), F32)
    for index, value in enumerate(values):
        out = jnp.where(lane == index, value, out)
    return out


def scatter_next_kernel(capacity, last, arrived, row_at, col_at, sigma, *refs):
    if last:
        previous, field, sides, sums, total = refs
    else:
        previous, (field, sides, sums, total) = None, refs
    levels, rows, cols = sigma.shape
    stride = capacity + 1
    gathered = jnp.concatenate(
        [arrived[at : at + 1] for at in range(capacity, arrived.shape[0], stride)], axis=0
    )
    added = jnp.sum(gathered, axis=0, keepdims=True)
    sums[...] = jnp.broadcast_to(added, (8, 128))

    group = 128 if last else 64

    def load(index):
        return load_group(index, group, capacity, row_at, col_at, arrived, stride, 0)

    scatter_into(
        total, load, row_at.shape[0], levels // 2 * rows, 2 * cols, group
    )
    extra = None
    if last:
        beta = lane_value(added, 1) / lane_value(added, 0)

        def extra(level):
            return beta * previous[level]

    sides[...] = pack_sides(put_field(total, sigma, field, extra))


def scatter_next(arrived, row_at, col_at, sigma, capacity, previous=None):
    levels, rows, cols = sigma.shape
    last = previous is not None
    shapes = [(levels, rows, cols), (rows, cols), (8, 128)]
    operands = [arrived, row_at, col_at, sigma] + ([previous] if last else [])
    out = pl.pallas_call(
        functools.partial(scatter_next_kernel, capacity, last),
        out_shape=[jax.ShapeDtypeStruct(shape, F32) for shape in shapes],
        in_specs=[VMEM] * len(operands),
        out_specs=[VMEM] * len(shapes),
        scratch_shapes=[pltpu.VMEM((levels // 2 * rows, 2 * cols), F32)],
        compiler_params=PARAMS,
        name="scatter_last" if last else "scatter_next",
    )(*operands)
    return out


def gather_from(fields, row_at, col_at, seen, table, group, wide):
    rows, cols = fields[0].shape
    half_rows, half_cols = len(fields) // 2 * rows, 2 * cols
    for level, field in enumerate(fields):
        high, low = parts(field.T)
        c, r = level % 2 * cols, level // 2 * rows
        table[c : c + cols, r : r + rows] = high
        table[c : c + cols, half_rows + r : half_rows + r + rows] = low
    row_iota = index_iota(half_rows)
    sublane = lax.broadcasted_iota(jnp.int32, (8, 128 * wide), 0)

    def step(index, carry):
        base = pl.multiple_of(index * group, group)
        row_block = row_at[pl.ds(base, group)]
        col_block = col_at[pl.ds(base, group)].astype(jnp.int32)
        found = []
        for j in range(0, group, wide):
            hot = jnp.concatenate(
                [one_hot(row_iota, row_block[i : i + 1]) for i in range(j, j + wide)], axis=1
            )
            hot = jnp.concatenate([hot, hot], axis=0)
            lines = jnp.dot(table[...], hot, preferred_element_type=F32)
            wanted = jnp.concatenate([col_block[i : i + 1] for i in range(j, j + wide)], axis=1)
            wanted = jnp.broadcast_to(wanted, (8, 128 * wide))
            tiles = [lines[i : i + 8] for i in range(0, half_cols, 8)]
            bit = 8
            while len(tiles) > 1:
                upper = (wanted & bit) != 0
                tiles = [
                    jnp.where(upper, tiles[i + 1], tiles[i]) for i in range(0, len(tiles), 2)
                ]
                bit = bit * 2
            value = jnp.sum(
                jnp.where((wanted & 7) == sublane, tiles[0], 0.0), axis=0, keepdims=True
            )
            found += [value[:, 128 * i : 128 * (i + 1)] for i in range(wide)]
        seen[pl.ds(base, group)] = jnp.concatenate(found, axis=0)
        return carry

    lax.fori_loop(0, row_at.shape[0] // group, step, 0)


def own_part(field, level, rows):
    inner = slice(EDGE + HALO, EDGE + HALO + rows)
    return pick_out(field[level, inner], field[level + 1, inner], level)


def total_of(pairs):
    added = None
    for left, right in pairs:
        term = left * right
        added = term if added is None else added + term
    return jnp.sum(added)


def observe_first_kernel(source, *refs):
    halo, weights, sigma, row_at, col_at = refs[:3], refs[3], refs[4], refs[5], refs[6]
    seen, right, image, sums, field, spare, table = refs[7:]
    levels, rows, cols = source.shape
    place(field, source, halo, halo[0].shape[0] - 1)
    clear_margins(spare)
    spare, field = smooth(field, spare, weights, 0, 80, True)
    right[...] = field[:, EDGE : EDGE + rows + 2 * HALO]
    own = [own_part(field, level, rows) for level in range(levels)]
    sums[...] = lanes([total_of([(value, value) for value in own])], 8)
    spare, field = smooth(field, spare, weights, 8, 72, True)
    fields = [sigma[level] * own_part(field, level, rows) for level in range(levels)]
    for level in range(levels):
        image[level] = fields[level]
    gather_from(fields, row_at, col_at, seen, table, 32, 4)


def observe_next_kernel(source, *refs):
    halo, weights, sigma, row_at, col_at = refs[:3], refs[3], refs[4], refs[5], refs[6]
    right, scalars = refs[7:9]
    seen, residual, image, sums, field, spare, table = refs[9:]
    levels, rows, cols = source.shape
    tall = rows + 2 * HALO
    norm, product = lane_value(scalars[0:1], 0), lane_value(scalars[0:1], 1)
    alpha = norm / (norm + product)
    place(field, source, halo, halo[0].shape[0] - 1)
    clear_margins(spare)
    spare, field = smooth(field, spare, weights, 0, 80, True)

    for tile in range(levels + 1):
        first = right[tile]
        field[tile, EDGE : EDGE + tall] = first - alpha * (first + field[tile, EDGE : EDGE + tall])
    own = [own_part(field, level, rows) for level in range(levels)]
    first = [pick_out(
            right[level, HALO : HALO + rows], right[level + 1, HALO : HALO + rows], level
        ) for level in range(levels)]
    for level in range(levels):
        residual[level] = own[level]
    sums[...] = lanes(
        [total_of([(value, value) for value in own]), total_of(list(zip(own, first)))], 8
    )
    spare, field = smooth(field, spare, weights, 8, 72, True)
    fields = [sigma[level] * own_part(field, level, rows) for level in range(levels)]
    for level in range(levels):
        image[level] = fields[level]
    gather_from(fields, row_at, col_at, seen, table, 64, 8)


def observe(source, halo, weights, sigma, row_at, col_at, right=None, scalars=None):
    levels, rows, cols = sigma.shape
    tall = rows + 2 * HALO
    slots = row_at.shape[0]
    first = right is None
    kept = (levels + 1, tall, cols) if first else (levels, rows, cols)
    shapes = [(slots, 128), kept, (levels, rows, cols), (8, 128)]
    operands = [source, *halo, weights, sigma, row_at, col_at]
    operands += [] if first else [right, scalars]
    return pl.pallas_call(
        observe_first_kernel if first else observe_next_kernel,
        out_shape=[jax.ShapeDtypeStruct(shape, F32) for shape in shapes],
        in_specs=[VMEM] * len(operands),
        out_specs=[VMEM] * len(shapes),
        scratch_shapes=[
            pltpu.VMEM((levels + 1, tall + 2 * EDGE, cols), F32),
            pltpu.VMEM((levels + 1, tall + 2 * EDGE, cols), F32),
            pltpu.VMEM(
                (2 * cols, levels * rows), BF16
            ),
        ],
        compiler_params=PARAMS,
        name="observe_first" if first else "observe_next",
    )(*operands)


def finish_kernel(source, *refs):
    halo, weights, right, residual_one, image_zero, image_one, scalars = refs[:3], *refs[3:9]
    increment, residual, field, spare = refs[9:]
    levels, rows, cols = source.shape
    norm_zero, norm_one, cross, product_zero, product_one, product_cross = [
        lane_value(scalars[0:1], index) for index in range(6)
    ]
    alpha_zero = norm_zero / (norm_zero + product_zero)
    beta = norm_one / norm_zero
    square = norm_one + 2.0 * beta * cross + beta * beta * norm_zero
    seen = product_one + 2.0 * beta * product_cross + beta * beta * product_zero
    alpha_one = norm_one / (square + seen)
    for level in range(levels):
        direction = image_one[level] + beta * image_zero[level]
        increment[level] = alpha_zero * image_zero[level] + alpha_one * direction
    place(field, source, halo, halo[0].shape[0] - 1)
    clear_margins(spare)
    spare, field = smooth(field, spare, weights, 8, 72, True)
    for level in range(levels):
        here = residual_one[level]
        direction = here + beta * pick_out(
            right[level, HALO : HALO + rows], right[level + 1, HALO : HALO + rows], level
        )
        image = direction + own_part(field, level, rows)
        residual[level] = here - alpha_one * image


def finish(source, halo, weights, right, residual_one, image_zero, image_one, scalars):
    levels, rows, cols = source.shape
    tall = rows + 2 * HALO
    return pl.pallas_call(
        finish_kernel,
        out_shape=[jax.ShapeDtypeStruct((levels, rows, cols), F32)] * 2,
        in_specs=[VMEM] * 10,
        out_specs=[VMEM] * 2,
        scratch_shapes=[pltpu.VMEM((levels + 1, tall + 2 * EDGE, cols), F32),
            pltpu.VMEM((levels + 1, tall + 2 * EDGE, cols), F32)],
        compiler_params=PARAMS,
        name="finish",
    )(source, *halo, weights, right, residual_one, image_zero, image_one, scalars)


def block_columns(values, weights, at):
    high, low = parts(values)
    first = jnp.concatenate([high, low, jnp.zeros((128 - 2 * GROUP, 128), BF16)], axis=0)
    second = jnp.concatenate([high, jnp.zeros((128 - GROUP, 128), BF16)], axis=0)
    right = jnp.concatenate([first, second], axis=1)
    lane = lane_of(128)
    column = jnp.where(lane < 2 * GROUP, lane % GROUP, GROUP)
    kept = jnp.zeros((128, 128), F32)
    for start in range(0, GROUP, 4):
        matrix = weights[at + start : at + start + 4].reshape(4 * 128, 128)
        left = jnp.concatenate(parts(matrix), axis=1)
        product = lax.dot_general(left, right, (((1,), (1,)), ((), ())), preferred_element_type=F32)
        for k in range(4):
            kept = jnp.where(column == start + k, product[k * 128 : (k + 1) * 128], kept)
    return kept


def turned(columns):
    rows = columns.T
    return rows[:GROUP] + rows[GROUP : 2 * GROUP]


def start_kernel(capacity, owner, cells, innovations, weights, mask, east, north, *refs):
    parcel, places, products, sides = refs[:4]
    count, held_cells, held_values, held_weights, held_mask, held_faces, held_sides = refs[4:11]
    columns, arrived, left = refs[11:]
    held = held_cells.shape[0]
    levels = mask.shape[0]
    steps = held // CHUNK
    moves = [
        (innovations, held_values),
        (cells, held_cells),
        (mask, held_mask),
        (east, held_faces.at[0]),
        (north, held_faces.at[1]),
    ]
    for step in range(steps):
        block = pl.ds(step * CHUNK, CHUNK)
        moves.append((weights.at[block], held_weights.at[block]))
    copies = [
        pltpu.make_async_copy(source, target, arrived.at[index])
        for index, (source, target) in enumerate(moves)
    ]
    for copy in copies[: 5 + AHEAD]:
        copy.start()
    parcel[...] = jnp.zeros_like(parcel)
    for index in range(count.shape[0]):
        count[index] = 0
    for index in range(held):
        target = owner[index]
        rank = count[target]
        count[target] = rank + 1
        places[index] = target * capacity + rank
        places[held + index] = target * (capacity + 1) + rank
    for copy in copies[2:5]:
        copy.wait()
    for index in range(2):
        fields = [held_mask[level].astype(F32) * held_faces[index, level] for level in range(levels)]
        for level in range(levels):
            held_faces[index, level] = fields[level]
        held_sides[index] = pack_sides(fields)
    returns = [
        pltpu.make_async_copy(held_faces, products, left.at[0]),
        pltpu.make_async_copy(held_sides, sides, left.at[1]),
    ]
    for copy in returns:
        copy.start()
    copies[0].wait()
    copies[1].wait()
    for first in range(0, held, GROUP):
        if first % CHUNK == 0:
            step = first // CHUNK
            copies[5 + step].wait()
            if step + AHEAD < steps:
                copies[5 + step + AHEAD].start()
        columns[first // GROUP] = block_columns(
            held_values[first : first + GROUP], held_weights, first
        )
    for first in range(0, held, GROUP):
        result = turned(columns[first // GROUP])
        cell_rows = held_cells[first : first + GROUP].astype(F32)
        for k in range(GROUP):
            at = places[first + k] + owner[first + k] * capacity
            parcel[pl.ds(at, 1), :] = cell_rows[k : k + 1]
            parcel[pl.ds(at + capacity, 1), :] = result[k : k + 1]
    for copy in returns:
        copy.wait()


def start(owner, cells, innovations, weights, mask, east, north, devices, capacity):
    held, width = cells.shape
    shapes = [(devices * 2 * capacity, width), (2 * held,), (2,) + mask.shape, (2,) + mask.shape[1:]]
    types = [F32, jnp.int32, F32, F32]
    return pl.pallas_call(
        functools.partial(start_kernel, capacity),
        out_shape=[jax.ShapeDtypeStruct(shape, kind) for shape, kind in zip(shapes, types)],
        in_specs=[SMEM] + [HBM] * 6,
        out_specs=[VMEM, SMEM, HBM, HBM],
        scratch_shapes=[
            pltpu.SMEM((devices,), jnp.int32),
            pltpu.VMEM((held, width), jnp.int32),
            pltpu.VMEM((held, width), F32),
            pltpu.VMEM((held, width, width), F32),
            pltpu.VMEM(mask.shape, jnp.int32),
            pltpu.VMEM((2,) + mask.shape, F32),
            pltpu.VMEM((2,) + mask.shape[1:], F32),
            pltpu.VMEM((held // GROUP, width, width), F32),
            pltpu.SemaphoreType.DMA((5 + held // CHUNK,)),
            pltpu.SemaphoreType.DMA((2,)),
        ],
        compiler_params=ROOMLESS,
        name="start",
    )(owner, cells, innovations, weights, mask, east, north)


def weigh_next_kernel(capacity, devices, last, places, returned, sums, weights, *refs):
    held = weights.shape[0]
    copies = []
    if last:
        sums_before, weighted_before, parcel, values, columns = refs
    else:
        parcel, weighted, values, columns, held_weights, arrived = refs
        for step in range(held // CHUNK):
            block = pl.ds(step * CHUNK, CHUNK)
            copies.append(
                pltpu.make_async_copy(
                    weights.at[block], held_weights.at[block], arrived.at[step]
                )
            )
        for copy in copies[:AHEAD]:
            copy.start()
        weights = held_weights
    parcel[...] = jnp.zeros_like(parcel)
    total = jnp.zeros((GROUP, 128), F32)
    total_cross = jnp.zeros((GROUP, 128), F32)
    for first in range(0, held, GROUP):
        here = jnp.concatenate(
            [returned[pl.ds(places[first + k], 1), :] for k in range(GROUP)], axis=0
        )
        values[first : first + GROUP] = here
        if copies and first % CHUNK == 0:
            step = first // CHUNK
            copies[step].wait()
            if step + AHEAD < len(copies):
                copies[step + AHEAD].start()
        columns[first // GROUP] = block_columns(here, weights, first)
    for first in range(0, held, GROUP):
        here = values[first : first + GROUP]
        result = turned(columns[first // GROUP])
        total += here * result
        if last:
            total_cross += here * weighted_before[first : first + GROUP]
        else:
            weighted[first : first + GROUP] = result
        for k in range(GROUP):
            parcel[pl.ds(places[held + first + k], 1), :] = result[k : k + 1]
    if last:
        scalars = [
            lane_value(sums_before[0:1], 0) / devices,
            lane_value(sums[0:1], 0),
            lane_value(sums[0:1], 1),
            lane_value(sums_before[0:1], 1) / devices,
            jnp.sum(total),
            jnp.sum(total_cross),
        ]
    else:
        scalars = [lane_value(sums[0:1], 0), jnp.sum(total)]
    row = lanes(scalars, 1)
    for target in range(devices):
        at = target * (capacity + 1) + capacity
        parcel[at : at + 1] = row


def weigh_next(places, returned, sums, weights, devices, capacity, before=None):
    held, width = weights.shape[:2]
    last = before is not None
    operands = [places, returned, sums, weights] + (list(before) if last else [])
    out_shape = [jax.ShapeDtypeStruct((devices * (capacity + 1), width), F32)]
    if not last:
        out_shape += [jax.ShapeDtypeStruct((held, width), F32)]
    return pl.pallas_call(
        functools.partial(weigh_next_kernel, capacity, devices, last),
        out_shape=out_shape,
        in_specs=[SMEM, VMEM, VMEM, VMEM if last else HBM] + [VMEM] * (len(operands) - 4),
        out_specs=[VMEM] * len(out_shape),
        scratch_shapes=[
            pltpu.VMEM((held, width), F32),
            pltpu.VMEM((held // GROUP, width, width), F32),
        ]
        + (
            []
            if last
            else [pltpu.VMEM(weights.shape, F32), pltpu.SemaphoreType.DMA((held // CHUNK,))]
        ),
        compiler_params=PARAMS if last else SNUG,
        name="weigh_last" if last else "weigh_next",
    )(*operands)


def swap(block):
    devices = lax.axis_size("lat") * lax.axis_size("lon")
    shares = block.reshape(devices, block.shape[0] // devices, 1, block.shape[1])
    got = lax.all_to_all(shares, ("lat", "lon"), split_axis=0, concat_axis=0, tiled=True)
    return got.reshape(block.shape)


def body(sigma, east_coef, north_coef, mask, innovations, cells, owner, obs_weights):
    devices = lax.axis_size("lat") * lax.axis_size("lon")
    held, width = cells.shape
    capacity = max(2, (2 * held + devices - 1) // devices)

    parcel, places, products, sides = start(
        owner.reshape(held),
        cells,
        innovations,
        obs_weights,
        mask,
        east_coef,
        north_coef,
        devices,
        capacity,
    )
    face_columns = exchange_columns(sides)
    arrived = swap(parcel)

    row_at, col_at, field, sides = scatter_first(arrived, sigma, capacity)
    face_columns, sides = lax.optimization_barrier((face_columns, sides))
    face_mixed, *face_rows = turn((products, *face_columns))
    mixed, down, up = turn((field, *exchange_columns(sides)), rows_ahead=tuple(face_rows))
    before, after = exchange_rows(down, up)
    weights = face_weights(products, (before, after, face_mixed))
    seen, right, image_zero, sums = observe(
        field, (before, after, mixed), weights, sigma, row_at, col_at
    )
    returned = swap(seen)
    parcel, weighted = weigh_next(places, returned, sums, obs_weights, devices, capacity)
    arrived = swap(parcel)

    field_zero, sides, scalars_zero = scatter_next(arrived, row_at, col_at, sigma, capacity)
    seen, residual_one, image_one, sums = observe(
        field_zero, exchange(field_zero, sides), weights, sigma, row_at, col_at, right, scalars_zero
    )
    returned = swap(seen)
    (parcel,) = weigh_next(
        places, returned, sums, obs_weights, devices, capacity, (scalars_zero, weighted)
    )
    arrived = swap(parcel)

    field, sides, scalars = scatter_next(arrived, row_at, col_at, sigma, capacity, field_zero)
    increment, residual = finish(
        field, exchange(field, sides), weights, right, residual_one, image_zero, image_one, scalars
    )
    return (increment, residual)


def solution(mesh):
    return jax.shard_map(
        body,
        mesh=mesh,
        in_specs=(
            P(None, "lat", "lon"),
            P(None, "lat", "lon"),
            P(None, "lat", "lon"),
            P(None, "lat", "lon"),
            P(("lat", "lon"), None),
            P(("lat", "lon"), None),
            P(("lat", "lon"), None),
            P(("lat", "lon"), None, None),
        ),
        out_specs=(P(None, "lat", "lon"), P(None, "lat", "lon")),
        check_vma=False,
    )
```

profile of v0, /device:TPU:8, one launch (start us, length us, event | category | flops | bytes accessed | tf_op | source)
XLA Modules:
  0.0 171.4 jit_solution(16401323290527616433)
XLA Ops:
  0.6 6.6 %start.1 = (f32[512,128]{1,0:T(8,128)}, s32[256]{0:T(256)}, f32[2,4,128,128]{3,2,1,0:T(8,128)}, f32[2,128,128]{2,1,0:T(8,128)}) custom-call(s32[128]{0:T(128)} %bitcast.29, s32[128,128]{1,0:T(8,128)} %cells.1, f32[128,128]{1,0:T(8,128)} %innovations.1, f32[128,128,128]{2,1,0:T(8,128)} %weights.5, s32[4,128,128]{2,1,0:T(8,128)} %mask.1, f32[4,128,128]{2,1,0:T(8,128)} %east.1, ...), custom_call_target="tpu_custom_call" | custom-call | tf_op jit(solution)/shard_map/start/pallas_call | solution.py:685
  7.3 6.0 %all-to-all-start = ((f32[32,16,1,128]{3,1,2,0:T(8,128)}), f32[32,16,1,128]{3,1,2,0:T(8,128)S(1)}, u32[]{:S(2)}, u32[]{:S(2)}) async-start(f32[32,16,1,128]{3,1,2,0:T(8,128)} %bitcast.28), calls=%async_computation | async-start | bytes 524288 | tf_op jit(solution)/shard_map/all_to_all | solution.py:794
  13.5 2.5 %collective-permute-start = (f32[2,128,128]{2,1,0:T(8,128)}, f32[2,128,128]{2,1,0:T(8,128)S(1)}, u32[]{:S(2)}, u32[]{:S(2)}) collective-permute-start(f32[2,128,128]{2,1,0:T(8,128)} %get-tuple-element.44), channel_id=1, source_target_pairs={{1,0},{2,1},{3,2},{4,3},{5,4},{6,5},{7,6},{0,7},{9,8},{10,9},{11,1... | collective-permute-start | bytes 393224 | tf_op jit(solution)/shard_map/ppermute | solution.py:81
  16.0 7.0 %all-to-all-done = f32[32,16,1,128]{3,1,2,0:T(8,128)S(1)} async-done(((f32[32,16,1,128]{3,1,2,0:T(8,128)}), f32[32,16,1,128]{3,1,2,0:T(8,128)S(1)}, u32[]{:S(2)}, u32[]{:S(2)}) %all-to-all-start) | async-done | bytes 262176 | tf_op jit(solution)/shard_map/all_to_all | solution.py:794
  23.1 9.9 %scatter_first.1 = (f32[256,128]{1,0:T(8,128)S(1)}, f32[256,128]{1,0:T(8,128)S(1)}, f32[4,128,128]{2,1,0:T(8,128)S(1)}, f32[128,128]{1,0:T(8,128)S(1)}) custom-call(f32[512,128]{1,0:T(8,128)S(1)} %bitcast.19, f32[4,128,128]{2,1,0:T(8,128)S(1)} %copy-done), custom_call_target="tpu_custom_call" | custom-call | tf_op jit(solution)/shard_map/scatter_first/pallas_call | solution.py:349
  33.1 2.6 %collective-permute-start.2 = (f32[128,128]{1,0:T(8,128)S(1)}, f32[128,128]{1,0:T(8,128)S(1)}, u32[]{:S(2)}, u32[]{:S(2)}) collective-permute-start(f32[128,128]{1,0:T(8,128)S(1)} %get-tuple-element.46), channel_id=1, source_target_pairs={{1,0},{2,1},{3,2},{4,3},{5,4},{6,5},{7,6},{0,7},{9,8},{10,9},{11,1... | collective-permute-start | bytes 196616 | tf_op jit(solution)/shard_map/ppermute | solution.py:81
  35.7 1.0 copy-done.1
  36.8 1.5 collective-permute-done.3.refs_2_
  39.1 2.3 %collective-permute-start.4 = (f32[3,5,16,128]{3,2,1,0:T(8,128)S(1)}, f32[3,5,16,128]{3,2,1,0:T(8,128)S(1)}, u32[]{:S(2)}, u32[]{:S(2)}) collective-permute-start(f32[3,5,16,128]{3,2,1,0:T(8,128)S(1)} %get-tuple-element.83), channel_id=1, source_target_pairs={{8,16},{16,8},{9,17},{17,9},{10,18},{18,10},{11,19},{19,11},{12,20... | collective-permute-start | bytes 368648 | tf_op jit(solution)/shard_map/ppermute | solution.py:109
  41.4 2.0 %collective-permute-done.5 = f32[3,5,16,128]{3,2,1,0:T(8,128)S(1)} collective-permute-done((f32[3,5,16,128]{3,2,1,0:T(8,128)S(1)}, f32[3,5,16,128]{3,2,1,0:T(8,128)S(1)}, u32[]{:S(2)}, u32[]{:S(2)}) %collective-permute-start.5) | collective-permute-done | bytes 122912 | tf_op jit(solution)/shard_map/ppermute | solution.py:106
  43.3 2.7 %collective-permute-done.4 = f32[3,5,16,128]{3,2,1,0:T(8,128)S(1)} collective-permute-done((f32[3,5,16,128]{3,2,1,0:T(8,128)S(1)}, f32[3,5,16,128]{3,2,1,0:T(8,128)S(1)}, u32[]{:S(2)}, u32[]{:S(2)}) %collective-permute-start.4) | collective-permute-done | bytes 122912 | tf_op jit(solution)/shard_map/ppermute | solution.py:109
  47.6 14.7 %observe_first.1 = (f32[256,128]{1,0:T(8,128)S(1)}, f32[5,160,128]{2,1,0:T(8,128)S(1)}, f32[4,128,128]{2,1,0:T(8,128)S(1)}, f32[8,128]{1,0:T(8,128)S(1)}) custom-call(f32[4,128,128]{2,1,0:T(8,128)S(1)} %get-tuple-element.43.refs_0_.source, f32[3,5,16,128]{3,2,1,0:T(8,128)S(1)} %get-tuple-element.81.before.refs_0_, ...), custom_call_target="tpu_custom_call" | custom-call | tf_op jit(solution)/shard_map/observe_first/pallas_call | solution.py:533
  62.4 9.6 %all_to_all.25 = f32[32,8,1,128]{3,1,2,0:T(8,128)S(1)} all-to-all(f32[32,8,1,128]{3,1,2,0:T(8,128)S(1)} %bitcast.26), channel_id=1, replica_groups=mesh['lat'=4,'lon'=8] {'lat','lon'}, dimensions={0} | all-to-all | bytes 262144 | tf_op jit(solution)/shard_map/all_to_all | solution.py:794
  72.0 5.7 %weigh_next.1 = (f32[288,128]{1,0:T(8,128)S(1)}, f32[128,128]{1,0:T(8,128)S(1)}) custom-call(s32[256]{0:T(256)S(1)} %copy-done.3, f32[256,128]{1,0:T(8,128)S(1)} %bitcast.24, f32[8,128]{1,0:T(8,128)S(1)} %get-tuple-element.59.sums, f32[128,128,128]{2,1,0:T(8,128)} %weights.5), custom_call_target="tpu_custom_call" | custom-call | tf_op jit(solution)/shard_map/weigh_next/pallas_call | solution.py:772
  77.7 10.2 %all_to_all.26 = f32[32,9,1,128]{3,2,1,0:T(1,128)S(1)} all-to-all(f32[32,9,1,128]{3,2,1,0:T(1,128)S(1)} %bitcast.25), channel_id=1, replica_groups=mesh['lat'=4,'lon'=8] {'lat','lon'}, dimensions={0} | all-to-all | bytes 294912 | tf_op jit(solution)/shard_map/all_to_all | solution.py:794
  87.9 9.6 %scatter_next.1 = (f32[4,128,128]{2,1,0:T(8,128)S(1)}, f32[128,128]{1,0:T(8,128)S(1)}, f32[8,128]{1,0:T(8,128)S(1)}) custom-call(f32[288,128]{1,0:T(8,128)S(1)} %bitcast.21, f32[256,128]{1,0:T(8,128)S(1)} %get-tuple-element.56.refs_5_.row_at, f32[256,128]{1,0:T(8,128)S(1)} %get-tuple-element.57.refs_6_.col_at, f32[4,128,128]{2,1,0:T(8,128)S(1)} %copy-done), custom_call_target="tpu_custom_call" | custom-call | tf_op jit(solution)/shard_map/scatter_next/pallas_call | solution.py:409
  97.6 2.6 %collective-permute-start.6 = (f32[128,128]{1,0:T(8,128)S(1)}, f32[128,128]{1,0:T(8,128)S(1)}, u32[]{:S(2)}, u32[]{:S(2)}) collective-permute-start(f32[128,128]{1,0:T(8,128)S(1)} %get-tuple-element.62), channel_id=1, source_target_pairs={{1,0},{2,1},{3,2},{4,3},{5,4},{6,5},{7,6},{0,7},{9,8},{10,9},{11,1... | collective-permute-start | bytes 196616 | tf_op jit(solution)/shard_map/ppermute | solution.py:81
  100.2 2.4 %collective-permute-done.7.refs_2_ = f32[128,128]{1,0:T(8,128)S(1)} collective-permute-done((f32[128,128]{1,0:T(8,128)S(1)}, f32[128,128]{1,0:T(8,128)S(1)}, u32[]{:S(2)}, u32[]{:S(2)}) %collective-permute-start.7) | collective-permute-done | bytes 65568 | tf_op jit(solution)/shard_map/ppermute | solution.py:80
  102.6 1.3 collective-permute-start.9
  103.9 2.4 %collective-permute-start.8 = (f32[1,5,16,128]{3,2,1,0:T(8,128)S(1)}, f32[1,5,16,128]{3,2,1,0:T(8,128)S(1)}, u32[]{:S(2)}, u32[]{:S(2)}) collective-permute-start(f32[1,5,16,128]{3,2,1,0:T(8,128)S(1)} %get-tuple-element.91), channel_id=1, source_target_pairs={{8,16},{16,8},{9,17},{17,9},{10,18},{18,10},{11,19},{19,11},{12,20... | collective-permute-start | bytes 122888 | tf_op jit(solution)/shard_map/ppermute | solution.py:109
  106.7 3.1 %collective-permute-done.8 = f32[1,5,16,128]{3,2,1,0:T(8,128)S(1)} collective-permute-done((f32[1,5,16,128]{3,2,1,0:T(8,128)S(1)}, f32[1,5,16,128]{3,2,1,0:T(8,128)S(1)}, u32[]{:S(2)}, u32[]{:S(2)}) %collective-permute-start.8) | collective-permute-done | bytes 40992 | tf_op jit(solution)/shard_map/ppermute | solution.py:109
  109.8 14.1 %observe_next.1 = (f32[256,128]{1,0:T(8,128)S(1)}, f32[4,128,128]{2,1,0:T(8,128)S(1)}, f32[4,128,128]{2,1,0:T(8,128)S(1)}, f32[8,128]{1,0:T(8,128)S(1)}) custom-call(f32[4,128,128]{2,1,0:T(8,128)S(1)} %get-tuple-element.61.refs_0_.source, f32[1,5,16,128]{3,2,1,0:T(8,128)S(1)} %get-tuple-element.89.refs_0_, f32[1,5,16,128]{3,2,1,0:T(8,128)S(1)} %get-tuple-element.88.refs_1_, ...), custom_call_target="tpu_custom_call" | custom-call | tf_op jit(solution)/shard_map/observe_next/pallas_call | solution.py:533
  123.9 9.3 %all_to_all.27 = f32[32,8,1,128]{3,1,2,0:T(8,128)S(1)} all-to-all(f32[32,8,1,128]{3,1,2,0:T(8,128)S(1)} %bitcast.27), channel_id=1, replica_groups=mesh['lat'=4,'lon'=8] {'lat','lon'}, dimensions={0} | all-to-all | bytes 262144 | tf_op jit(solution)/shard_map/all_to_all | solution.py:794
  133.3 3.1 %weigh_last.1 = f32[288,128]{1,0:T(8,128)S(1)} custom-call(s32[256]{0:T(256)S(1)} %copy-done.3, f32[256,128]{1,0:T(8,128)S(1)} %bitcast.23, f32[8,128]{1,0:T(8,128)S(1)} %get-tuple-element.69.sums, f32[128,128,128]{2,1,0:T(8,128)S(1)} %bitcast.18, f32[8,128]{1,0:T(8,128)S(1)} %get-tuple-element.67.refs_8_.refs_0_, f32[128,128]{1,0:T(8,128)S(1)} %get-tuple-element.70.refs_1_), custom_call_target="tpu_custom_call" | custom-call | tf_op jit(solution)/shard_map/weigh_last/pallas_call | solution.py:772
  136.4 10.2 %all_to_all.28 = f32[32,9,1,128]{3,2,1,0:T(1,128)S(1)} all-to-all(f32[32,9,1,128]{3,2,1,0:T(1,128)S(1)} %bitcast.22), channel_id=1, replica_groups=mesh['lat'=4,'lon'=8] {'lat','lon'}, dimensions={0} | all-to-all | bytes 294912 | tf_op jit(solution)/shard_map/all_to_all | solution.py:794
  146.6 9.4 %scatter_last.1 = (f32[4,128,128]{2,1,0:T(8,128)S(1)}, f32[128,128]{1,0:T(8,128)S(1)}, f32[8,128]{1,0:T(8,128)S(1)}) custom-call(f32[288,128]{1,0:T(8,128)S(1)} %bitcast.20, f32[256,128]{1,0:T(8,128)S(1)} %get-tuple-element.56.refs_5_.row_at, f32[256,128]{1,0:T(8,128)S(1)} %get-tuple-element.57.refs_6_.col_at, f32[4,128,128]{2,1,0:T(8,128)S(1)} %copy-done, ...), custom_call_target="tpu_custom_call" | custom-call | tf_op jit(solution)/shard_map/scatter_last/pallas_call | solution.py:409
  156.1 2.6 %collective-permute-start.10 = (f32[128,128]{1,0:T(8,128)S(1)}, f32[128,128]{1,0:T(8,128)S(1)}, u32[]{:S(2)}, u32[]{:S(2)}) collective-permute-start(f32[128,128]{1,0:T(8,128)S(1)} %get-tuple-element.72), channel_id=1, source_target_pairs={{1,0},{2,1},{3,2},{4,3},{5,4},{6,5},{7,6},{0,7},{9,8},{10,9},{11,1... | collective-permute-start | bytes 196616 | tf_op jit(solution)/shard_map/ppermute | solution.py:81
  158.7 2.4 %collective-permute-done.11.refs_2_ = f32[128,128]{1,0:T(8,128)S(1)} collective-permute-done((f32[128,128]{1,0:T(8,128)S(1)}, f32[128,128]{1,0:T(8,128)S(1)}, u32[]{:S(2)}, u32[]{:S(2)}) %collective-permute-start.11) | collective-permute-done | bytes 65568 | tf_op jit(solution)/shard_map/ppermute | solution.py:80
  161.1 1.3 collective-permute-start.13
  162.5 2.4 %collective-permute-start.12 = (f32[1,5,16,128]{3,2,1,0:T(8,128)S(1)}, f32[1,5,16,128]{3,2,1,0:T(8,128)S(1)}, u32[]{:S(2)}, u32[]{:S(2)}) collective-permute-start(f32[1,5,16,128]{3,2,1,0:T(8,128)S(1)} %get-tuple-element.87), channel_id=1, source_target_pairs={{8,16},{16,8},{9,17},{17,9},{10,18},{18,10},{11,19},{19,11},{12,20... | collective-permute-start | bytes 122888 | tf_op jit(solution)/shard_map/ppermute | solution.py:109
  165.2 3.2 %collective-permute-done.12 = f32[1,5,16,128]{3,2,1,0:T(8,128)S(1)} collective-permute-done((f32[1,5,16,128]{3,2,1,0:T(8,128)S(1)}, f32[1,5,16,128]{3,2,1,0:T(8,128)S(1)}, u32[]{:S(2)}, u32[]{:S(2)}) %collective-permute-start.12) | collective-permute-done | bytes 40992 | tf_op jit(solution)/shard_map/ppermute | solution.py:109
  168.4 3.0 %finish.1 = (f32[4,128,128]{2,1,0:T(8,128)}, f32[4,128,128]{2,1,0:T(8,128)}) custom-call(f32[4,128,128]{2,1,0:T(8,128)S(1)} %get-tuple-element.71.refs_0_.source, f32[1,5,16,128]{3,2,1,0:T(8,128)S(1)} %get-tuple-element.85.refs_0_, f32[1,5,16,128]{3,2,1,0:T(8,128)S(1)} %get-tuple-element.84.refs_1_, f32[128,128]{1,0:T(8,128)S(1)} %get-tuple-element.75.refs_2_, ...), custom_call_target="tpu_custom_call" | custom-call | tf_op jit(solution)/shard_map/finish/pallas_call | solution.py:580
  (35 shorter events, 3.5 us)
Async XLA Ops:
  0.6 22.4 %copy-start = (f32[4,128,128]{2,1,0:T(8,128)S(1)}, f32[4,128,128]{2,1,0:T(8,128)}, u32[]{:S(2)}) copy-start(f32[4,128,128]{2,1,0:T(8,128)} %sigma.5) | copy-start | bytes 786436
  7.3 64.7 %copy-start.3 = (s32[256]{0:T(256)S(1)}, s32[256]{0:T(256)}, u32[]{:S(2)}) copy-start(s32[256]{0:T(256)} %get-tuple-element.41.places) | copy-start | bytes 3076
  7.3 15.8 %all-to-all-start = ((f32[32,16,1,128]{3,1,2,0:T(8,128)}), f32[32,16,1,128]{3,1,2,0:T(8,128)S(1)}, u32[]{:S(2)}, u32[]{:S(2)}) async-start(f32[32,16,1,128]{3,1,2,0:T(8,128)} %bitcast.28), calls=%async_computation | async-start | bytes 524288 | tf_op jit(solution)/shard_map/all_to_all | solution.py:794
  13.3 19.7 %collective-permute-start.1 = (f32[2,128,128]{2,1,0:T(8,128)}, f32[2,128,128]{2,1,0:T(8,128)S(1)}, u32[]{:S(2)}, u32[]{:S(2)}) collective-permute-start(f32[2,128,128]{2,1,0:T(8,128)} %get-tuple-element.44), channel_id=1, source_target_pairs={{0,1},{1,2},{2,3},{3,4},{4,5},{5,6},{6,7},{7,0},{8,9},{9,10},{10,1... | collective-permute-start | bytes 393224 | tf_op jit(solution)/shard_map/ppermute | solution.py:80
  13.5 19.5 %collective-permute-start = (f32[2,128,128]{2,1,0:T(8,128)}, f32[2,128,128]{2,1,0:T(8,128)S(1)}, u32[]{:S(2)}, u32[]{:S(2)}) collective-permute-start(f32[2,128,128]{2,1,0:T(8,128)} %get-tuple-element.44), channel_id=1, source_target_pairs={{1,0},{2,1},{3,2},{4,3},{5,4},{6,5},{7,6},{0,7},{9,8},{10,9},{11,1... | collective-permute-start | bytes 393224 | tf_op jit(solution)/shard_map/ppermute | solution.py:81
  33.0 5.3 %collective-permute-start.3 = (f32[128,128]{1,0:T(8,128)S(1)}, f32[128,128]{1,0:T(8,128)S(1)}, u32[]{:S(2)}, u32[]{:S(2)}) collective-permute-start(f32[128,128]{1,0:T(8,128)S(1)} %get-tuple-element.46), channel_id=1, source_target_pairs={{0,1},{1,2},{2,3},{3,4},{4,5},{5,6},{6,7},{7,0},{8,9},{9,10},{10,1... | collective-permute-start | bytes 196616 | tf_op jit(solution)/shard_map/ppermute | solution.py:80
  33.1 5.2 %collective-permute-start.2 = (f32[128,128]{1,0:T(8,128)S(1)}, f32[128,128]{1,0:T(8,128)S(1)}, u32[]{:S(2)}, u32[]{:S(2)}) collective-permute-start(f32[128,128]{1,0:T(8,128)S(1)} %get-tuple-element.46), channel_id=1, source_target_pairs={{1,0},{2,1},{3,2},{4,3},{5,4},{6,5},{7,6},{0,7},{9,8},{10,9},{11,1... | collective-permute-start | bytes 196616 | tf_op jit(solution)/shard_map/ppermute | solution.py:81
  35.7 1.0 copy-start.1
  38.4 4.9 %collective-permute-start.5 = (f32[3,5,16,128]{3,2,1,0:T(8,128)S(1)}, f32[3,5,16,128]{3,2,1,0:T(8,128)S(1)}, u32[]{:S(2)}, u32[]{:S(2)}) collective-permute-start(f32[3,5,16,128]{3,2,1,0:T(8,128)S(1)} %get-tuple-element.82), channel_id=1, source_target_pairs={{0,8},{16,24},{8,0},{24,16},{1,9},{17,25},{9,1},{25,17},{2,10},{18... | collective-permute-start | bytes 368648 | tf_op jit(solution)/shard_map/ppermute | solution.py:106
  39.1 6.9 %collective-permute-start.4 = (f32[3,5,16,128]{3,2,1,0:T(8,128)S(1)}, f32[3,5,16,128]{3,2,1,0:T(8,128)S(1)}, u32[]{:S(2)}, u32[]{:S(2)}) collective-permute-start(f32[3,5,16,128]{3,2,1,0:T(8,128)S(1)} %get-tuple-element.83), channel_id=1, source_target_pairs={{8,16},{16,8},{9,17},{17,9},{10,18},{18,10},{11,19},{19,11},{12,20... | collective-permute-start | bytes 368648 | tf_op jit(solution)/shard_map/ppermute | solution.py:109
  46.0 1.0 copy-start.2
  47.6 85.7 %slice-start = ((s8[8388608]{0:T(1024)(128)(4,1)}), s8[4194304]{0:T(1024)(128)(4,1)S(1)}, s32[]{:S(2)}) async-start(s8[8388608]{0:T(1024)(128)(4,1)} %bitcast.17), calls=%async_computation.5 | async-start | bytes 8388608
  72.0 61.3 %slice-start.1 = ((s8[8388608]{0:T(1024)(128)(4,1)}), s8[4194304]{0:T(1024)(128)(4,1)S(1)}, s32[]{:S(2)}) async-start(s8[8388608]{0:T(1024)(128)(4,1)} %bitcast.17), calls=%async_computation.6 | async-start | bytes 8388608
  97.5 5.1 %collective-permute-start.7 = (f32[128,128]{1,0:T(8,128)S(1)}, f32[128,128]{1,0:T(8,128)S(1)}, u32[]{:S(2)}, u32[]{:S(2)}) collective-permute-start(f32[128,128]{1,0:T(8,128)S(1)} %get-tuple-element.62), channel_id=1, source_target_pairs={{0,1},{1,2},{2,3},{3,4},{4,5},{5,6},{6,7},{7,0},{8,9},{9,10},{10,1... | collective-permute-start | bytes 196616 | tf_op jit(solution)/shard_map/ppermute | solution.py:80
  97.6 5.0 %collective-permute-start.6 = (f32[128,128]{1,0:T(8,128)S(1)}, f32[128,128]{1,0:T(8,128)S(1)}, u32[]{:S(2)}, u32[]{:S(2)}) collective-permute-start(f32[128,128]{1,0:T(8,128)S(1)} %get-tuple-element.62), channel_id=1, source_target_pairs={{1,0},{2,1},{3,2},{4,3},{5,4},{6,5},{7,6},{0,7},{9,8},{10,9},{11,1... | collective-permute-start | bytes 196616 | tf_op jit(solution)/shard_map/ppermute | solution.py:81
  102.6 4.1 %collective-permute-start.9 = (f32[1,5,16,128]{3,2,1,0:T(8,128)S(1)}, f32[1,5,16,128]{3,2,1,0:T(8,128)S(1)}, u32[]{:S(2)}, u32[]{:S(2)}) collective-permute-start(f32[1,5,16,128]{3,2,1,0:T(8,128)S(1)} %get-tuple-element.90), channel_id=1, source_target_pairs={{0,8},{16,24},{8,0},{24,16},{1,9},{17,25},{9,1},{25,17},{2,10},{18... | collective-permute-start | bytes 122888 | tf_op jit(solution)/shard_map/ppermute | solution.py:106
  103.9 5.9 %collective-permute-start.8 = (f32[1,5,16,128]{3,2,1,0:T(8,128)S(1)}, f32[1,5,16,128]{3,2,1,0:T(8,128)S(1)}, u32[]{:S(2)}, u32[]{:S(2)}) collective-permute-start(f32[1,5,16,128]{3,2,1,0:T(8,128)S(1)} %get-tuple-element.91), channel_id=1, source_target_pairs={{8,16},{16,8},{9,17},{17,9},{10,18},{18,10},{11,19},{19,11},{12,20... | collective-permute-start | bytes 122888 | tf_op jit(solution)/shard_map/ppermute | solution.py:109
  156.0 5.1 %collective-permute-start.11 = (f32[128,128]{1,0:T(8,128)S(1)}, f32[128,128]{1,0:T(8,128)S(1)}, u32[]{:S(2)}, u32[]{:S(2)}) collective-permute-start(f32[128,128]{1,0:T(8,128)S(1)} %get-tuple-element.72), channel_id=1, source_target_pairs={{0,1},{1,2},{2,3},{3,4},{4,5},{5,6},{6,7},{7,0},{8,9},{9,10},{10,1... | collective-permute-start | bytes 196616 | tf_op jit(solution)/shard_map/ppermute | solution.py:80
  156.1 5.0 %collective-permute-start.10 = (f32[128,128]{1,0:T(8,128)S(1)}, f32[128,128]{1,0:T(8,128)S(1)}, u32[]{:S(2)}, u32[]{:S(2)}) collective-permute-start(f32[128,128]{1,0:T(8,128)S(1)} %get-tuple-element.72), channel_id=1, source_target_pairs={{1,0},{2,1},{3,2},{4,3},{5,4},{6,5},{7,6},{0,7},{9,8},{10,9},{11,1... | collective-permute-start | bytes 196616 | tf_op jit(solution)/shard_map/ppermute | solution.py:81
  161.1 4.1 %collective-permute-start.13 = (f32[1,5,16,128]{3,2,1,0:T(8,128)S(1)}, f32[1,5,16,128]{3,2,1,0:T(8,128)S(1)}, u32[]{:S(2)}, u32[]{:S(2)}) collective-permute-start(f32[1,5,16,128]{3,2,1,0:T(8,128)S(1)} %get-tuple-element.86), channel_id=1, source_target_pairs={{0,8},{16,24},{8,0},{24,16},{1,9},{17,25},{9,1},{25,17},{2,10},{18... | collective-permute-start | bytes 122888 | tf_op jit(solution)/shard_map/ppermute | solution.py:106
  162.5 5.9 %collective-permute-start.12 = (f32[1,5,16,128]{3,2,1,0:T(8,128)S(1)}, f32[1,5,16,128]{3,2,1,0:T(8,128)S(1)}, u32[]{:S(2)}, u32[]{:S(2)}) collective-permute-start(f32[1,5,16,128]{3,2,1,0:T(8,128)S(1)} %get-tuple-element.87), channel_id=1, source_target_pairs={{8,16},{16,8},{9,17},{17,9},{10,18},{18,10},{11,19},{19,11},{12,20... | collective-permute-start | bytes 122888 | tf_op jit(solution)/shard_map/ppermute | solution.py:109
where the time goes:
time: 172 us; the launch traced here: 171 us
  Pallas kernels  76.7 us (45%)
  blocking collectives  39.4 us (23%)
  starting transfers between devices  27.3 us (16%)
  waiting for transfers between devices  24.9 us (14%)
  local copies, waits for them, and re-layouts  2.1 us (1%)
    all_to_all x4, blocking collectives, swap(): lax.all_to_all(shares, ('lat', 'lon'), split_axis=0, concat_axis=0, tiled...  39.4 us
    pallas_call x2, Pallas kernels, observe(): pl.pallas_call(observe_first_kernel if first else observe_next_kernel, ou...  28.8 us
    pallas_call x2, Pallas kernels, scatter_next(): pl.pallas_call(functools.partial(scatter_next_kernel, capacity, last), ou...  18.9 us
    ppermute x4, starting transfers between devices, exchange_columns(): from_east = lax.ppermute(sides, 'lon', [(to, at) for at, to in east])  10.4 us
    pallas_call x1, Pallas kernels, scatter_first(): pl.pallas_call(functools.partial(scatter_first_kernel, capacity), out_sha...  9.9 us
    ppermute x3, waiting for transfers between devices, exchange_rows(): lax.ppermute(jnp.where(even, up, down), 'lat', second + [(to, at) for at,...  8.97 us
    pallas_call x2, Pallas kernels, weigh_next(): pl.pallas_call(functools.partial(weigh_next_kernel, capacity, devices, la...  8.78 us
    ppermute x3, starting transfers between devices, exchange_rows(): lax.ppermute(jnp.where(even, up, down), 'lat', second + [(to, at) for at,...  7.11 us
  transfers between devices with their start and end apart: 15, of which 10 were waited for; matrix products, arithmetic and copies ran while one was open for 0% of the time, Pallas kernels for 6%

commit v1 on v0

--- a/solution.py
+++ b/solution.py
@@ -43,12 +43,27 @@
         start = 2 * HALO * level
         turned = pltpu.roll(field, (start + HALO) % 128, 1)
         packed = jnp.where((lane >= start) & (lane < start + 2 * HALO), turned, packed)
-    return packed
-
-
-def turn_kernel(count, *refs):
-    sources, extra = refs[: 3 * count], refs[3 * count : len(refs) - count - 2]
-    *mixed, down, up = refs[len(refs) - count - 2 :]
+    half = packed.shape[0] // 2
+    low, high = packed[:half], packed[half:]
+    western = lane[:half] % (2 * HALO) < HALO
+    return (
+        jnp.where(western, low, pltpu.roll(high, HALO, 1)),
+        jnp.where(western, pltpu.roll(low, 128 - HALO, 1), high),
+    )
+
+
+def unpack_sides(from_east, from_west):
+    western = lane_of(from_east.shape[0]) % (2 * HALO) < HALO
+    low = jnp.where(western, from_west, pltpu.roll(from_east, HALO, 1))
+    high = jnp.where(western, pltpu.roll(from_west, 128 - HALO, 1), from_east)
+    return jnp.concatenate([low, high], axis=0)
+
+
+def turn_kernel(count, ahead, *refs):
+    sources, extra = refs[: 3 * count], refs[3 * count : 3 * count + ahead]
+    *mixed, down, up = refs[3 * count + ahead : 4 * count + ahead + 2]
+    for kept in refs[4 * count + ahead + 2 :]:
+        kept[...] = sources[0][...]
     row = 0
     if extra:
         row = extra[0].shape[0]
@@ -57,9 +72,8 @@
     for index in range(count):
         fields, from_east, from_west = sources[3 * index : 3 * index + 3]
         levels, rows, _ = fields.shape[-3:]
-        western = lane_of(rows) % (2 * HALO) < HALO
         for at in [(i,) for i in range(fields.shape[0])] if len(fields.shape) == 4 else [()]:
-            sides = jnp.where(western, from_west[at + (...,)], from_east[at + (...,)])
+            sides = unpack_sides(from_east[at + (...,)], from_west[at + (...,)])
             mixed[index][at + (...,)] = sides
             for level in range(levels):
                 down[row, level] = fields[at + (level, slice(rows - HALO, rows))]
@@ -77,19 +91,20 @@
 def exchange_columns(sides):
     wide = lax.axis_size("lon")
     east = [(i, (i + 1) % wide) for i in range(wide)]
-    from_west = lax.ppermute(sides, "lon", east)
-    from_east = lax.ppermute(sides, "lon", [(to, at) for at, to in east])
+    from_west = lax.ppermute(sides[0], "lon", east)
+    from_east = lax.ppermute(sides[1], "lon", [(to, at) for at, to in east])
     return from_east, from_west
 
 
-def turn(*groups, rows_ahead=()):
+def turn(*groups, rows_ahead=(), keep=False):
     levels, rows, cols = groups[0][0].shape[-3:]
-    shapes = [sides.shape for _, sides, _ in groups]
+    shapes = [fields.shape[:-3] + (rows, cols) for fields, _, _ in groups]
     total = sum(fields.shape[0] if fields.ndim == 4 else 1 for fields, _, _ in groups)
     total += rows_ahead[0].shape[0] if rows_ahead else 0
     shapes += [(total, levels + 1, HALO, cols)] * 2
+    shapes += [groups[0][0].shape] if keep else []
     return pl.pallas_call(
-        functools.partial(turn_kernel, len(groups)),
+        functools.partial(turn_kernel, len(groups), len(rows_ahead)),
         out_shape=[jax.ShapeDtypeStruct(shape, F32) for shape in shapes],
         in_specs=[VMEM] * (3 * len(groups) + len(rows_ahead)),
         out_specs=[VMEM] * len(shapes),
@@ -325,7 +340,7 @@
 
 
 def scatter_first_kernel(capacity, arrived, sigma, row_at, col_at, field, *refs):
-    sides, total = refs
+    eastward, westward, total = refs
     levels, rows, cols = sigma.shape
     stride = 2 * capacity
     cells = jnp.concatenate(
@@ -339,13 +354,13 @@
         return load_group(index, 64, capacity, row_at, col_at, arrived, stride, capacity)
 
     scatter_into(total, load, row_at.shape[0], levels // 2 * rows, 2 * cols, 64)
-    sides[...] = pack_sides(put_field(total, sigma, field))
+    eastward[...], westward[...] = pack_sides(put_field(total, sigma, field))
 
 
 def scatter_first(arrived, sigma, capacity):
     levels, rows, cols = sigma.shape
     slots = arrived.shape[0] // 2
-    shapes = [(slots, 128), (slots, 128), (levels, rows, cols), (rows, cols)]
+    shapes = [(slots, 128), (slots, 128), (levels, rows, cols)] + [(rows // 2, cols)] * 2
     out = pl.pallas_call(
         functools.partial(scatter_first_kernel, capacity),
         out_shape=[jax.ShapeDtypeStruct(shape, F32) for shape in shapes],
@@ -372,9 +387,9 @@
 
 def scatter_next_kernel(capacity, last, arrived, row_at, col_at, sigma, *refs):
     if last:
-        previous, field, sides, sums, total = refs
+        previous, field, eastward, westward, sums, total = refs
     else:
-        previous, (field, sides, sums, total) = None, refs
+        previous, (field, eastward, westward, sums, total) = None, refs
     levels, rows, cols = sigma.shape
     stride = capacity + 1
     gathered = jnp.concatenate(
@@ -398,13 +413,13 @@
         def extra(level):
             return beta * previous[level]
 
-    sides[...] = pack_sides(put_field(total, sigma, field, extra))
+    eastward[...], westward[...] = pack_sides(put_field(total, sigma, field, extra))
 
 
 def scatter_next(arrived, row_at, col_at, sigma, capacity, previous=None):
     levels, rows, cols = sigma.shape
     last = previous is not None
-    shapes = [(levels, rows, cols), (rows, cols), (8, 128)]
+    shapes = [(levels, rows, cols)] + [(rows // 2, cols)] * 2 + [(8, 128)]
     operands = [arrived, row_at, col_at, sigma] + ([previous] if last else [])
     out = pl.pallas_call(
         functools.partial(scatter_next_kernel, capacity, last),
@@ -500,7 +515,7 @@
     alpha = norm / (norm + product)
     place(field, source, halo, halo[0].shape[0] - 1)
     clear_margins(spare)
-    spare, field = smooth(field, spare, weights, 0, 80, True)
+    spare, field = smooth(field, spare, weights, 0, 160, True)
 
     for tile in range(levels + 1):
         first = right[tile]
@@ -514,7 +529,7 @@
     sums[...] = lanes(
         [total_of([(value, value) for value in own]), total_of(list(zip(own, first)))], 8
     )
-    spare, field = smooth(field, spare, weights, 8, 72, True)
+    spare, field = smooth(field, spare, weights, 8, 144, True)
     fields = [sigma[level] * own_part(field, level, rows) for level in range(levels)]
     for level in range(levels):
         image[level] = fields[level]
@@ -564,7 +579,7 @@
         increment[level] = alpha_zero * image_zero[level] + alpha_one * direction
     place(field, source, halo, halo[0].shape[0] - 1)
     clear_margins(spare)
-    spare, field = smooth(field, spare, weights, 8, 72, True)
+    spare, field = smooth(field, spare, weights, 8, 144, True)
     for level in range(levels):
         here = residual_one[level]
         direction = here + beta * pick_out(
@@ -612,9 +627,9 @@
 
 
 def start_kernel(capacity, owner, cells, innovations, weights, mask, east, north, *refs):
-    parcel, places, products, sides = refs[:4]
-    count, held_cells, held_values, held_weights, held_mask, held_faces, held_sides = refs[4:11]
-    columns, arrived, left = refs[11:]
+    parcel, places, products, eastward, westward = refs[:5]
+    count, held_cells, held_values, held_weights, held_mask, held_faces, held_sides = refs[5:12]
+    columns, arrived, left = refs[12:]
     held = held_cells.shape[0]
     levels = mask.shape[0]
     steps = held // CHUNK
@@ -649,10 +664,11 @@
         fields = [held_mask[level].astype(F32) * held_faces[index, level] for level in range(levels)]
         for level in range(levels):
             held_faces[index, level] = fields[level]
-        held_sides[index] = pack_sides(fields)
+        held_sides[0, index], held_sides[1, index] = pack_sides(fields)
     returns = [
         pltpu.make_async_copy(held_faces, products, left.at[0]),
-        pltpu.make_async_copy(held_sides, sides, left.at[1]),
+        pltpu.make_async_copy(held_sides.at[0], eastward, left.at[1]),
+        pltpu.make_async_copy(held_sides.at[1], westward, left.at[2]),
     ]
     for copy in returns:
         copy.start()
@@ -680,13 +696,15 @@
 
 def start(owner, cells, innovations, weights, mask, east, north, devices, capacity):
     held, width = cells.shape
-    shapes = [(devices * 2 * capacity, width), (2 * held,), (2,) + mask.shape, (2,) + mask.shape[1:]]
-    types = [F32, jnp.int32, F32, F32]
+    rows, cols = mask.shape[1:]
+    shapes = [(devices * 2 * capacity, width), (2 * held,), (2,) + mask.shape]
+    shapes += [(2, rows // 2, cols)] * 2
+    types = [F32, jnp.int32, F32, F32, F32]
     return pl.pallas_call(
         functools.partial(start_kernel, capacity),
         out_shape=[jax.ShapeDtypeStruct(shape, kind) for shape, kind in zip(shapes, types)],
         in_specs=[SMEM] + [HBM] * 6,
-        out_specs=[VMEM, SMEM, HBM, HBM],
+        out_specs=[VMEM, SMEM, HBM, HBM, HBM],
         scratch_shapes=[
             pltpu.SMEM((devices,), jnp.int32),
             pltpu.VMEM((held, width), jnp.int32),
@@ -694,10 +712,10 @@
             pltpu.VMEM((held, width, width), F32),
             pltpu.VMEM(mask.shape, jnp.int32),
             pltpu.VMEM((2,) + mask.shape, F32),
-            pltpu.VMEM((2,) + mask.shape[1:], F32),
+            pltpu.VMEM((2, 2, rows // 2, cols), F32),
             pltpu.VMEM((held // GROUP, width, width), F32),
             pltpu.SemaphoreType.DMA((5 + held // CHUNK,)),
-            pltpu.SemaphoreType.DMA((2,)),
+            pltpu.SemaphoreType.DMA((3,)),
         ],
         compiler_params=ROOMLESS,
         name="start",
@@ -800,7 +818,7 @@
     held, width = cells.shape
     capacity = max(2, (2 * held + devices - 1) // devices)
 
-    parcel, places, products, sides = start(
+    parcel, places, products, *sides = start(
         owner.reshape(held),
         cells,
         innovations,
@@ -814,9 +832,9 @@
     face_columns = exchange_columns(sides)
     arrived = swap(parcel)
 
-    row_at, col_at, field, sides = scatter_first(arrived, sigma, capacity)
+    row_at, col_at, field, *sides = scatter_first(arrived, sigma, capacity)
     face_columns, sides = lax.optimization_barrier((face_columns, sides))
-    face_mixed, *face_rows = turn((products, *face_columns))
+    face_mixed, *face_rows, products = turn((products, *face_columns), keep=True)
     mixed, down, up = turn((field, *exchange_columns(sides)), rows_ahead=tuple(face_rows))
     before, after = exchange_rows(down, up)
     weights = face_weights(products, (before, after, face_mixed))
@@ -827,7 +845,7 @@
     parcel, weighted = weigh_next(places, returned, sums, obs_weights, devices, capacity)
     arrived = swap(parcel)
 
-    field_zero, sides, scalars_zero = scatter_next(arrived, row_at, col_at, sigma, capacity)
+    field_zero, *sides, scalars_zero = scatter_next(arrived, row_at, col_at, sigma, capacity)
     seen, residual_one, image_one, sums = observe(
         field_zero, exchange(field_zero, sides), weights, sigma, row_at, col_at, right, scalars_zero
     )
@@ -837,7 +855,7 @@
     )
     arrived = swap(parcel)
 
-    field, sides, scalars = scatter_next(arrived, row_at, col_at, sigma, capacity, field_zero)
+    field, *sides, scalars = scatter_next(arrived, row_at, col_at, sigma, capacity, field_zero)
     increment, residual = finish(
         field, exchange(field, sides), weights, right, residual_one, image_zero, image_one, scalars
     )

time: 172 us -> 170 us (0.988)
  starting transfers between devices: 27.3 us -> 21.8 us
  waiting for transfers between devices: 24.9 us -> 29.5 us
    ppermute x8, starting transfers between devices: 10.8 us -> 3.85 us  [the longest x4 3.17 us: exchange_columns(): from_east = lax.ppermute(sides[1], 'lon', [(to, at) for at, to in east])]
    ppermute x8, waiting for transfers between devices: 6.29 us -> 10.9 us  [the longest x4 7.63 us: exchange_columns(): from_west = lax.ppermute(sides[0], 'lon', east)]
  transfers between devices with their start and end apart: 15 -> 15, of which waited for: 10 -> 12; matrix products, arithmetic and copies ran while one was open for 0% -> 0% of each run, Pallas kernels for 6% -> 6%
where the time goes in v1:
time: 170 us; the launch traced here: 169 us
  Pallas kernels  76 us (45%)
  blocking collectives  40.1 us (24%)
  waiting for transfers between devices  29.5 us (17%)
  starting transfers between devices  21.8 us (13%)
    all_to_all x4, blocking collectives, swap(): lax.all_to_all(shares, ('lat', 'lon'), split_axis=0, concat_axis=0, tiled...  40.1 us
    pallas_call x2, Pallas kernels, observe(): pl.pallas_call(observe_first_kernel if first else observe_next_kernel, ou...  28 us
    pallas_call x2, Pallas kernels, scatter_next(): pl.pallas_call(functools.partial(scatter_next_kernel, capacity, last), ou...  19.1 us
    pallas_call x1, Pallas kernels, scatter_first(): pl.pallas_call(functools.partial(scatter_first_kernel, capacity), out_sha...  9.98 us
    ppermute x3, waiting for transfers between devices, exchange_rows(): lax.ppermute(jnp.where(even, up, down), 'lat', second + [(to, at) for at,...  9.86 us
    pallas_call x2, Pallas kernels, weigh_next(): pl.pallas_call(functools.partial(weigh_next_kernel, capacity, devices, la...  8.79 us
    ppermute x4, waiting for transfers between devices, exchange_columns(): from_west = lax.ppermute(sides[0], 'lon', east)  7.63 us
    all_to_all x1, waiting for transfers between devices, swap(): lax.all_to_all(shares, ('lat', 'lon'), split_axis=0, concat_axis=0, tiled...  7.57 us
  transfers between devices with their start and end apart: 15, of which 12 were waited for; matrix products, arithmetic and copies ran while one was open for 0% of the time, Pallas kernels for 6%

profile of v1, /device:TPU:8, one launch (start us, length us, event | category | flops | bytes accessed | tf_op | source)
XLA Modules:
  0.0 169.4 jit_solution(8912666925776759020)
XLA Ops:
  0.6 6.6 %start.1 = (f32[512,128]{1,0:T(8,128)}, s32[256]{0:T(256)}, f32[2,4,128,128]{3,2,1,0:T(8,128)}, f32[2,64,128]{2,1,0:T(8,128)}, f32[2,64,128]{2,1,0:T(8,128)}) custom-call(s32[128]{0:T(128)} %bitcast.29, s32[128,128]{1,0:T(8,128)} %cells.1, f32[128,128]{1,0:T(8,128)} %innovations.1, f32[128,128,128]{2,1,0:T(8,128)} %weights.5, s32[4,128,128]{2,1,0:T(8,128)} %mask.1, ...), custom_call_target="tpu_custom_call" | custom-call | tf_op jit(solution)/shard_map/start/pallas_call | solution.py:703
  7.3 6.0 %all-to-all-start = ((f32[32,16,1,128]{3,1,2,0:T(8,128)}), f32[32,16,1,128]{3,1,2,0:T(8,128)S(1)}, u32[]{:S(2)}, u32[]{:S(2)}) async-start(f32[32,16,1,128]{3,1,2,0:T(8,128)} %bitcast.28), calls=%async_computation | async-start | bytes 524288 | tf_op jit(solution)/shard_map/all_to_all | solution.py:812
  13.4 2.2 %collective-permute-start = (f32[2,64,128]{2,1,0:T(8,128)}, f32[2,64,128]{2,1,0:T(8,128)S(1)}, u32[]{:S(2)}, u32[]{:S(2)}) collective-permute-start(f32[2,64,128]{2,1,0:T(8,128)} %get-tuple-element.50), channel_id=1, source_target_pairs={{1,0},{2,1},{3,2},{4,3},{5,4},{6,5},{7,6},{0,7},{9,8},{10,9},{11,1... | collective-permute-start | bytes 196616 | tf_op jit(solution)/shard_map/ppermute | solution.py:95
  15.5 7.6 %all-to-all-done = f32[32,16,1,128]{3,1,2,0:T(8,128)S(1)} async-done(((f32[32,16,1,128]{3,1,2,0:T(8,128)}), f32[32,16,1,128]{3,1,2,0:T(8,128)S(1)}, u32[]{:S(2)}, u32[]{:S(2)}) %all-to-all-start) | async-done | bytes 262176 | tf_op jit(solution)/shard_map/all_to_all | solution.py:812
  23.1 10.0 %scatter_first.1 = (f32[256,128]{1,0:T(8,128)S(1)}, f32[256,128]{1,0:T(8,128)S(1)}, f32[4,128,128]{2,1,0:T(8,128)S(1)}, f32[64,128]{1,0:T(8,128)S(1)}, f32[64,128]{1,0:T(8,128)S(1)}) custom-call(f32[512,128]{1,0:T(8,128)S(1)} %bitcast.19, f32[4,128,128]{2,1,0:T(8,128)S(1)} %copy-done), custom_call_target="tpu_custom_call" | custom-call | tf_op jit(solution)/shard_map/scatter_first/pallas_call | solution.py:364
  33.7 1.0 copy-done.1
  34.8 2.6 %collective-permute-done.3.refs_2_ = f32[64,128]{1,0:T(8,128)S(1)} collective-permute-done((f32[64,128]{1,0:T(8,128)S(1)}, f32[64,128]{1,0:T(8,128)S(1)}, u32[]{:S(2)}, u32[]{:S(2)}) %collective-permute-start.3) | collective-permute-done | bytes 32800 | tf_op jit(solution)/shard_map/ppermute | solution.py:94
  37.6 1.7 collective-permute-start.5
  39.2 2.4 %collective-permute-start.4 = (f32[3,5,16,128]{3,2,1,0:T(8,128)S(1)}, f32[3,5,16,128]{3,2,1,0:T(8,128)S(1)}, u32[]{:S(2)}, u32[]{:S(2)}) collective-permute-start(f32[3,5,16,128]{3,2,1,0:T(8,128)S(1)} %get-tuple-element.95), channel_id=1, source_target_pairs={{8,16},{16,8},{9,17},{17,9},{10,18},{18,10},{11,19},{19,11},{12,20... | collective-permute-start | bytes 368648 | tf_op jit(solution)/shard_map/ppermute | solution.py:124
  41.7 0.8 collective-permute-done.5
  42.5 3.5 %collective-permute-done.4 = f32[3,5,16,128]{3,2,1,0:T(8,128)S(1)} collective-permute-done((f32[3,5,16,128]{3,2,1,0:T(8,128)S(1)}, f32[3,5,16,128]{3,2,1,0:T(8,128)S(1)}, u32[]{:S(2)}, u32[]{:S(2)}) %collective-permute-start.4) | collective-permute-done | bytes 122912 | tf_op jit(solution)/shard_map/ppermute | solution.py:124
  46.6 14.7 %observe_first.1 = (f32[256,128]{1,0:T(8,128)S(1)}, f32[5,160,128]{2,1,0:T(8,128)S(1)}, f32[4,128,128]{2,1,0:T(8,128)S(1)}, f32[8,128]{1,0:T(8,128)S(1)}) custom-call(f32[4,128,128]{2,1,0:T(8,128)S(1)} %get-tuple-element.49.refs_0_.source, f32[3,5,16,128]{3,2,1,0:T(8,128)S(1)} %get-tuple-element.93.before.refs_0_, ...), custom_call_target="tpu_custom_call" | custom-call | tf_op jit(solution)/shard_map/observe_first/pallas_call | solution.py:548
  61.4 9.8 %all_to_all.25 = f32[32,8,1,128]{3,1,2,0:T(8,128)S(1)} all-to-all(f32[32,8,1,128]{3,1,2,0:T(8,128)S(1)} %bitcast.26), channel_id=1, replica_groups=mesh['lat'=4,'lon'=8] {'lat','lon'}, dimensions={0} | all-to-all | bytes 262144 | tf_op jit(solution)/shard_map/all_to_all | solution.py:812
  71.2 5.7 %weigh_next.1 = (f32[288,128]{1,0:T(8,128)S(1)}, f32[128,128]{1,0:T(8,128)S(1)}) custom-call(s32[256]{0:T(256)S(1)} %copy-done.2, f32[256,128]{1,0:T(8,128)S(1)} %bitcast.24, f32[8,128]{1,0:T(8,128)S(1)} %get-tuple-element.69.sums, f32[128,128,128]{2,1,0:T(8,128)} %weights.5), custom_call_target="tpu_custom_call" | custom-call | tf_op jit(solution)/shard_map/weigh_next/pallas_call | solution.py:790
  76.9 10.2 %all_to_all.26 = f32[32,9,1,128]{3,2,1,0:T(1,128)S(1)} all-to-all(f32[32,9,1,128]{3,2,1,0:T(1,128)S(1)} %bitcast.25), channel_id=1, replica_groups=mesh['lat'=4,'lon'=8] {'lat','lon'}, dimensions={0} | all-to-all | bytes 294912 | tf_op jit(solution)/shard_map/all_to_all | solution.py:812
  87.1 9.7 %scatter_next.1 = (f32[4,128,128]{2,1,0:T(8,128)S(1)}, f32[64,128]{1,0:T(8,128)S(1)}, f32[64,128]{1,0:T(8,128)S(1)}, f32[8,128]{1,0:T(8,128)S(1)}) custom-call(f32[288,128]{1,0:T(8,128)S(1)} %bitcast.21, f32[256,128]{1,0:T(8,128)S(1)} %get-tuple-element.66.refs_5_.row_at, f32[256,128]{1,0:T(8,128)S(1)} %get-tuple-element.67.refs_6_.col_at, ...), custom_call_target="tpu_custom_call" | custom-call | tf_op jit(solution)/shard_map/scatter_next/pallas_call | solution.py:424
  97.3 1.6 collective-permute-done.6.refs_1_
  99.0 2.5 %collective-permute-done.7.refs_2_ = f32[64,128]{1,0:T(8,128)S(1)} collective-permute-done((f32[64,128]{1,0:T(8,128)S(1)}, f32[64,128]{1,0:T(8,128)S(1)}, u32[]{:S(2)}, u32[]{:S(2)}) %collective-permute-start.7) | collective-permute-done | bytes 32800 | tf_op jit(solution)/shard_map/ppermute | solution.py:94
  101.6 1.4 collective-permute-start.9
  103.0 2.5 %collective-permute-start.8 = (f32[1,5,16,128]{3,2,1,0:T(8,128)S(1)}, f32[1,5,16,128]{3,2,1,0:T(8,128)S(1)}, u32[]{:S(2)}, u32[]{:S(2)}) collective-permute-start(f32[1,5,16,128]{3,2,1,0:T(8,128)S(1)} %get-tuple-element.103), channel_id=1, source_target_pairs={{8,16},{16,8},{9,17},{17,9},{10,18},{18,10},{11,19},{19,11},{12,20... | collective-permute-start | bytes 122888 | tf_op jit(solution)/shard_map/ppermute | solution.py:124
  105.7 3.2 %collective-permute-done.8 = f32[1,5,16,128]{3,2,1,0:T(8,128)S(1)} collective-permute-done((f32[1,5,16,128]{3,2,1,0:T(8,128)S(1)}, f32[1,5,16,128]{3,2,1,0:T(8,128)S(1)}, u32[]{:S(2)}, u32[]{:S(2)}) %collective-permute-start.8) | collective-permute-done | bytes 40992 | tf_op jit(solution)/shard_map/ppermute | solution.py:124
  108.9 13.3 %observe_next.1 = (f32[256,128]{1,0:T(8,128)S(1)}, f32[4,128,128]{2,1,0:T(8,128)S(1)}, f32[4,128,128]{2,1,0:T(8,128)S(1)}, f32[8,128]{1,0:T(8,128)S(1)}) custom-call(f32[4,128,128]{2,1,0:T(8,128)S(1)} %get-tuple-element.71.refs_0_.source, f32[1,5,16,128]{3,2,1,0:T(8,128)S(1)} %get-tuple-element.101.refs_0_, ...), custom_call_target="tpu_custom_call" | custom-call | tf_op jit(solution)/shard_map/observe_next/pallas_call | solution.py:548
  122.2 9.8 %all_to_all.27 = f32[32,8,1,128]{3,1,2,0:T(8,128)S(1)} all-to-all(f32[32,8,1,128]{3,1,2,0:T(8,128)S(1)} %bitcast.27), channel_id=1, replica_groups=mesh['lat'=4,'lon'=8] {'lat','lon'}, dimensions={0} | all-to-all | bytes 262144 | tf_op jit(solution)/shard_map/all_to_all | solution.py:812
  131.9 3.1 %weigh_last.1 = f32[288,128]{1,0:T(8,128)S(1)} custom-call(s32[256]{0:T(256)S(1)} %copy-done.2, f32[256,128]{1,0:T(8,128)S(1)} %bitcast.23, f32[8,128]{1,0:T(8,128)S(1)} %get-tuple-element.80.sums, f32[128,128,128]{2,1,0:T(8,128)S(1)} %bitcast.18, f32[8,128]{1,0:T(8,128)S(1)} %get-tuple-element.78.refs_8_.refs_0_, f32[128,128]{1,0:T(8,128)S(1)} %get-tuple-element.81.refs_1_), custom_call_target="tpu_custom_call" | custom-call | tf_op jit(solution)/shard_map/weigh_last/pallas_call | solution.py:790
  135.1 10.2 %all_to_all.28 = f32[32,9,1,128]{3,2,1,0:T(1,128)S(1)} all-to-all(f32[32,9,1,128]{3,2,1,0:T(1,128)S(1)} %bitcast.22), channel_id=1, replica_groups=mesh['lat'=4,'lon'=8] {'lat','lon'}, dimensions={0} | all-to-all | bytes 294912 | tf_op jit(solution)/shard_map/all_to_all | solution.py:812
  145.3 9.4 %scatter_last.1 = (f32[4,128,128]{2,1,0:T(8,128)S(1)}, f32[64,128]{1,0:T(8,128)S(1)}, f32[64,128]{1,0:T(8,128)S(1)}, f32[8,128]{1,0:T(8,128)S(1)}) custom-call(f32[288,128]{1,0:T(8,128)S(1)} %bitcast.20, f32[256,128]{1,0:T(8,128)S(1)} %get-tuple-element.66.refs_5_.row_at, f32[256,128]{1,0:T(8,128)S(1)} %get-tuple-element.67.refs_6_.col_at, ...), custom_call_target="tpu_custom_call" | custom-call | tf_op jit(solution)/shard_map/scatter_last/pallas_call | solution.py:424
  155.3 1.7 collective-permute-done.10.refs_1_
  157.0 2.5 %collective-permute-done.11.refs_2_ = f32[64,128]{1,0:T(8,128)S(1)} collective-permute-done((f32[64,128]{1,0:T(8,128)S(1)}, f32[64,128]{1,0:T(8,128)S(1)}, u32[]{:S(2)}, u32[]{:S(2)}) %collective-permute-start.11) | collective-permute-done | bytes 32800 | tf_op jit(solution)/shard_map/ppermute | solution.py:94
  159.5 1.4 collective-permute-start.13
  160.9 2.5 %collective-permute-start.12 = (f32[1,5,16,128]{3,2,1,0:T(8,128)S(1)}, f32[1,5,16,128]{3,2,1,0:T(8,128)S(1)}, u32[]{:S(2)}, u32[]{:S(2)}) collective-permute-start(f32[1,5,16,128]{3,2,1,0:T(8,128)S(1)} %get-tuple-element.99), channel_id=1, source_target_pairs={{8,16},{16,8},{9,17},{17,9},{10,18},{18,10},{11,19},{19,11},{12,20... | collective-permute-start | bytes 122888 | tf_op jit(solution)/shard_map/ppermute | solution.py:124
  163.6 3.2 %collective-permute-done.12 = f32[1,5,16,128]{3,2,1,0:T(8,128)S(1)} collective-permute-done((f32[1,5,16,128]{3,2,1,0:T(8,128)S(1)}, f32[1,5,16,128]{3,2,1,0:T(8,128)S(1)}, u32[]{:S(2)}, u32[]{:S(2)}) %collective-permute-start.12) | collective-permute-done | bytes 40992 | tf_op jit(solution)/shard_map/ppermute | solution.py:124
  166.8 2.6 %finish.1 = (f32[4,128,128]{2,1,0:T(8,128)}, f32[4,128,128]{2,1,0:T(8,128)}) custom-call(f32[4,128,128]{2,1,0:T(8,128)S(1)} %get-tuple-element.82.refs_0_.source, f32[1,5,16,128]{3,2,1,0:T(8,128)S(1)} %get-tuple-element.97.refs_0_, f32[1,5,16,128]{3,2,1,0:T(8,128)S(1)} %get-tuple-element.96.refs_1_, f32[128,128]{1,0:T(8,128)S(1)} %get-tuple-element.87.refs_2_, ...), custom_call_target="tpu_custom_call" | custom-call | tf_op jit(solution)/shard_map/finish/pallas_call | solution.py:595
  (33 shorter events, 3.0 us)
Async XLA Ops:
  0.6 22.5 %copy-start = (f32[4,128,128]{2,1,0:T(8,128)S(1)}, f32[4,128,128]{2,1,0:T(8,128)}, u32[]{:S(2)}) copy-start(f32[4,128,128]{2,1,0:T(8,128)} %sigma.5) | copy-start | bytes 786436
  7.3 63.9 %copy-start.2 = (s32[256]{0:T(256)S(1)}, s32[256]{0:T(256)}, u32[]{:S(2)}) copy-start(s32[256]{0:T(256)} %get-tuple-element.47.places) | copy-start | bytes 3076
  7.3 15.8 %all-to-all-start = ((f32[32,16,1,128]{3,1,2,0:T(8,128)}), f32[32,16,1,128]{3,1,2,0:T(8,128)S(1)}, u32[]{:S(2)}, u32[]{:S(2)}) async-start(f32[32,16,1,128]{3,1,2,0:T(8,128)} %bitcast.28), calls=%async_computation | async-start | bytes 524288 | tf_op jit(solution)/shard_map/all_to_all | solution.py:812
  13.4 19.7 %collective-permute-start = (f32[2,64,128]{2,1,0:T(8,128)}, f32[2,64,128]{2,1,0:T(8,128)S(1)}, u32[]{:S(2)}, u32[]{:S(2)}) collective-permute-start(f32[2,64,128]{2,1,0:T(8,128)} %get-tuple-element.50), channel_id=1, source_target_pairs={{1,0},{2,1},{3,2},{4,3},{5,4},{6,5},{7,6},{0,7},{9,8},{10,9},{11,1... | collective-permute-start | bytes 196616 | tf_op jit(solution)/shard_map/ppermute | solution.py:95
  15.5 17.6 %collective-permute-start.1 = (f32[2,64,128]{2,1,0:T(8,128)}, f32[2,64,128]{2,1,0:T(8,128)S(1)}, u32[]{:S(2)}, u32[]{:S(2)}) collective-permute-start(f32[2,64,128]{2,1,0:T(8,128)} %get-tuple-element.51), channel_id=1, source_target_pairs={{0,1},{1,2},{2,3},{3,4},{4,5},{5,6},{6,7},{7,0},{8,9},{9,10},{10,1... | collective-permute-start | bytes 196616 | tf_op jit(solution)/shard_map/ppermute | solution.py:94
  33.1 1.7 %collective-permute-start.2 = (f32[64,128]{1,0:T(8,128)S(1)}, f32[64,128]{1,0:T(8,128)S(1)}, u32[]{:S(2)}, u32[]{:S(2)}) collective-permute-start(f32[64,128]{1,0:T(8,128)S(1)} %get-tuple-element.54), channel_id=1, source_target_pairs={{1,0},{2,1},{3,2},{4,3},{5,4},{6,5},{7,6},{0,7},{9,8},{10,9},{11,1... | collective-permute-start | bytes 98312 | tf_op jit(solution)/shard_map/ppermute | solution.py:95
  33.2 4.3 %collective-permute-start.3 = (f32[64,128]{1,0:T(8,128)S(1)}, f32[64,128]{1,0:T(8,128)S(1)}, u32[]{:S(2)}, u32[]{:S(2)}) collective-permute-start(f32[64,128]{1,0:T(8,128)S(1)} %get-tuple-element.55), channel_id=1, source_target_pairs={{0,1},{1,2},{2,3},{3,4},{4,5},{5,6},{6,7},{7,0},{8,9},{9,10},{10,1... | collective-permute-start | bytes 98312 | tf_op jit(solution)/shard_map/ppermute | solution.py:94
  33.7 1.0 copy-start.1
  37.6 4.9 %collective-permute-start.5 = (f32[3,5,16,128]{3,2,1,0:T(8,128)S(1)}, f32[3,5,16,128]{3,2,1,0:T(8,128)S(1)}, u32[]{:S(2)}, u32[]{:S(2)}) collective-permute-start(f32[3,5,16,128]{3,2,1,0:T(8,128)S(1)} %get-tuple-element.94), channel_id=1, source_target_pairs={{0,8},{16,24},{8,0},{24,16},{1,9},{17,25},{9,1},{25,17},{2,10},{18... | collective-permute-start | bytes 368648 | tf_op jit(solution)/shard_map/ppermute | solution.py:121
  39.2 6.8 %collective-permute-start.4 = (f32[3,5,16,128]{3,2,1,0:T(8,128)S(1)}, f32[3,5,16,128]{3,2,1,0:T(8,128)S(1)}, u32[]{:S(2)}, u32[]{:S(2)}) collective-permute-start(f32[3,5,16,128]{3,2,1,0:T(8,128)S(1)} %get-tuple-element.95), channel_id=1, source_target_pairs={{8,16},{16,8},{9,17},{17,9},{10,18},{18,10},{11,19},{19,11},{12,20... | collective-permute-start | bytes 368648 | tf_op jit(solution)/shard_map/ppermute | solution.py:124
  46.6 85.3 %slice-start = ((s8[8388608]{0:T(1024)(128)(4,1)}), s8[4194304]{0:T(1024)(128)(4,1)S(1)}, s32[]{:S(2)}) async-start(s8[8388608]{0:T(1024)(128)(4,1)} %bitcast.17), calls=%async_computation.5 | async-start | bytes 8388608
  71.2 60.8 %slice-start.1 = ((s8[8388608]{0:T(1024)(128)(4,1)}), s8[4194304]{0:T(1024)(128)(4,1)S(1)}, s32[]{:S(2)}) async-start(s8[8388608]{0:T(1024)(128)(4,1)} %bitcast.17), calls=%async_computation.6 | async-start | bytes 8388608
  96.8 2.2 %collective-permute-start.6 = (f32[64,128]{1,0:T(8,128)S(1)}, f32[64,128]{1,0:T(8,128)S(1)}, u32[]{:S(2)}, u32[]{:S(2)}) collective-permute-start(f32[64,128]{1,0:T(8,128)S(1)} %get-tuple-element.72), channel_id=1, source_target_pairs={{1,0},{2,1},{3,2},{4,3},{5,4},{6,5},{7,6},{0,7},{9,8},{10,9},{11,1... | collective-permute-start | bytes 98312 | tf_op jit(solution)/shard_map/ppermute | solution.py:95
  97.2 4.2 %collective-permute-start.7 = (f32[64,128]{1,0:T(8,128)S(1)}, f32[64,128]{1,0:T(8,128)S(1)}, u32[]{:S(2)}, u32[]{:S(2)}) collective-permute-start(f32[64,128]{1,0:T(8,128)S(1)} %get-tuple-element.73), channel_id=1, source_target_pairs={{0,1},{1,2},{2,3},{3,4},{4,5},{5,6},{6,7},{7,0},{8,9},{9,10},{10,1... | collective-permute-start | bytes 98312 | tf_op jit(solution)/shard_map/ppermute | solution.py:94
  101.6 4.1 %collective-permute-start.9 = (f32[1,5,16,128]{3,2,1,0:T(8,128)S(1)}, f32[1,5,16,128]{3,2,1,0:T(8,128)S(1)}, u32[]{:S(2)}, u32[]{:S(2)}) collective-permute-start(f32[1,5,16,128]{3,2,1,0:T(8,128)S(1)} %get-tuple-element.102), channel_id=1, source_target_pairs={{0,8},{16,24},{8,0},{24,16},{1,9},{17,25},{9,1},{25,17},{2,10},{18... | collective-permute-start | bytes 122888 | tf_op jit(solution)/shard_map/ppermute | solution.py:121
  103.0 5.9 %collective-permute-start.8 = (f32[1,5,16,128]{3,2,1,0:T(8,128)S(1)}, f32[1,5,16,128]{3,2,1,0:T(8,128)S(1)}, u32[]{:S(2)}, u32[]{:S(2)}) collective-permute-start(f32[1,5,16,128]{3,2,1,0:T(8,128)S(1)} %get-tuple-element.103), channel_id=1, source_target_pairs={{8,16},{16,8},{9,17},{17,9},{10,18},{18,10},{11,19},{19,11},{12,20... | collective-permute-start | bytes 122888 | tf_op jit(solution)/shard_map/ppermute | solution.py:124
  154.7 2.2 %collective-permute-start.10 = (f32[64,128]{1,0:T(8,128)S(1)}, f32[64,128]{1,0:T(8,128)S(1)}, u32[]{:S(2)}, u32[]{:S(2)}) collective-permute-start(f32[64,128]{1,0:T(8,128)S(1)} %get-tuple-element.83), channel_id=1, source_target_pairs={{1,0},{2,1},{3,2},{4,3},{5,4},{6,5},{7,6},{0,7},{9,8},{10,9},{11,1... | collective-permute-start | bytes 98312 | tf_op jit(solution)/shard_map/ppermute | solution.py:95
  155.2 4.2 %collective-permute-start.11 = (f32[64,128]{1,0:T(8,128)S(1)}, f32[64,128]{1,0:T(8,128)S(1)}, u32[]{:S(2)}, u32[]{:S(2)}) collective-permute-start(f32[64,128]{1,0:T(8,128)S(1)} %get-tuple-element.84), channel_id=1, source_target_pairs={{0,1},{1,2},{2,3},{3,4},{4,5},{5,6},{6,7},{7,0},{8,9},{9,10},{10,1... | collective-permute-start | bytes 98312 | tf_op jit(solution)/shard_map/ppermute | solution.py:94
  159.5 4.1 %collective-permute-start.13 = (f32[1,5,16,128]{3,2,1,0:T(8,128)S(1)}, f32[1,5,16,128]{3,2,1,0:T(8,128)S(1)}, u32[]{:S(2)}, u32[]{:S(2)}) collective-permute-start(f32[1,5,16,128]{3,2,1,0:T(8,128)S(1)} %get-tuple-element.98), channel_id=1, source_target_pairs={{0,8},{16,24},{8,0},{24,16},{1,9},{17,25},{9,1},{25,17},{2,10},{18... | collective-permute-start | bytes 122888 | tf_op jit(solution)/shard_map/ppermute | solution.py:121
  160.9 5.9 %collective-permute-start.12 = (f32[1,5,16,128]{3,2,1,0:T(8,128)S(1)}, f32[1,5,16,128]{3,2,1,0:T(8,128)S(1)}, u32[]{:S(2)}, u32[]{:S(2)}) collective-permute-start(f32[1,5,16,128]{3,2,1,0:T(8,128)S(1)} %get-tuple-element.99), channel_id=1, source_target_pairs={{8,16},{16,8},{9,17},{17,9},{10,18},{18,10},{11,19},{19,11},{12,20... | collective-permute-start | bytes 122888 | tf_op jit(solution)/shard_map/ppermute | solution.py:124
